TPU v7x, 512 devices: a whole 4x8x8 slice. The times are simulated.
512 devices in a mesh: row: 8 (over y), col: 8 (over x, z_hi), tp: 8 (over z_lo, core).
Axes of the slice: x: 4, y: 8, z: 8 (z_hi: 2, z_lo: 4; z = z_hi * 4 + z_lo), core: 2. Of those that a mesh axis runs over, the one named last changes fastest.
Arguments:
- act_one: bfloat16 [8, 8, 256, 8192], P('row', 'col', None, 'tp'), may hold values from -6 to 6
- residual: bfloat16 [8, 8, 256, 2048], P('row', 'col', None, 'tp'), may hold values from -6 to 6
- upstream: bfloat16 [8, 8, 256, 8192], P('row', 'col', None, 'tp'), may hold values from -6 to 6
- stream_grad: bfloat16 [8, 8, 256, 256], P('row', 'col'), may hold values from -6 to 6
- token_ids: int32 [8, 8, 256], P('row', 'col'), may hold values from 0 to 31999, as said below
- shard_counts: int32 [8, 8], P('row', 'col'), may hold values from 4096 to 106807
- out_one: bfloat16 [8, 8192, 2048], P('col', 'tp', 'row'), may hold values from -6 to 6
- in_two: bfloat16 [8, 8192, 2048], P('row', 'tp', 'col'), may hold values from -6 to 6
- out_one_moment: float32 [8, 8192, 256], P('col', 'tp', 'row'), may hold values from -3 to 3
- in_two_moment: float32 [8, 8192, 256], P('row', 'tp', 'col'), may hold values from -3 to 3
Outputs:
- out_one_new: float32 [8, 8192, 256], P('col', 'tp', 'row')
- out_one_moment_new: float32 [8, 8192, 256], P('col', 'tp', 'row')
- in_two_new: float32 [8, 8192, 256], P('row', 'tp', 'col')
- in_two_moment_new: float32 [8, 8192, 256], P('row', 'tp', 'col')
Inputs may be any that keep to these rules, and one draw needn't show every extreme that they name: `token_ids`: id 0 marks padding and appears only at the end of a path's tokens.
All inputs are finite; a program needn't handle non-finite values.
Results may differ from a plain program's by a relative error of at most 0.017.
Values may be sent and summed in bfloat16 or wider, within the bound.
A program may use at most 64 MiB of HBM per device.

v0:
```python
import math

import jax
import jax.numpy as jnp
from jax import lax
from jax.sharding import PartitionSpec as P

D = 2048
H = 8192
COLS = 256


inner_rate = 4.0
outer_rate = 0.7
momentum_decay = 0.9


def pick_columns(matrix, groups):
    rows = matrix.shape[0]
    wide = matrix.shape[1]
    return matrix.reshape(rows, groups, wide // groups)[:, :, : COLS // groups].reshape(rows, COLS)


def rounded(values):
    return lax.optimization_barrier(values.astype(jnp.bfloat16)).astype(jnp.float32)


def outer_step(storage, moment, summed, total, share):
    piece = storage[:, :share].astype(jnp.float32)
    delta = summed / total
    moment_new = momentum_decay * moment + delta
    fresh = piece - outer_rate * (delta + momentum_decay * moment_new)
    return (fresh[None], moment_new[None])


def on_device(
    act_one,
    residual,
    upstream,
    stream_grad,
    token_ids,
    shard_counts,
    out_one,
    in_two,
    out_one_moment,
    in_two_moment,
):
    scale_model = 1.0 / math.sqrt(D)
    scale_hidden = 1.0 / math.sqrt(H)
    act_rows = act_one[0, 0]
    resid_rows = residual[0, 0]
    keep = (token_ids[0, 0] != 0)[:, None]
    up_rows = jnp.where(keep, upstream[0, 0], jnp.zeros_like(upstream[0, 0]))
    stream_rows = jnp.where(keep, stream_grad[0, 0], jnp.zeros_like(stream_grad[0, 0]))
    first_store = out_one[0]
    second_store = in_two[0]
    n_rows = lax.axis_size("row")
    n_cols = lax.axis_size("col")
    row_index = lax.axis_index("row")
    col_index = lax.axis_index("col")
    partial_value = rounded(
        jnp.dot(
            act_rows,
            lax.all_gather(first_store, "row", axis=1, tiled=True),
            preferred_element_type=jnp.float32,
        )
        * scale_hidden
    )
    summed = lax.psum(partial_value.astype(jnp.bfloat16), "tp").astype(jnp.float32)
    resid_all = lax.all_gather(resid_rows, "tp", axis=1, tiled=True)
    stream_new = (resid_all.astype(jnp.float32) + summed).astype(jnp.bfloat16)
    second_weight = lax.all_gather(second_store, "col", axis=1, tiled=True)
    pre_second = (
        jnp.einsum("td,hd->th", stream_new, second_weight, preferred_element_type=jnp.float32)
        * scale_model
    )
    squash = jax.nn.sigmoid(pre_second)
    slope = (up_rows.astype(jnp.float32) * squash * (1.0 + pre_second * (1.0 - squash))).astype(
        jnp.bfloat16
    )
    grad_two = (
        jnp.einsum(
            "th,tc->hc", slope, pick_columns(stream_new, n_cols), preferred_element_type=jnp.float32
        )
        * scale_model
    )
    carried_part = rounded(
        jnp.dot(slope, pick_columns(second_weight, n_rows), preferred_element_type=jnp.float32)
        * scale_model
    )
    carried = lax.psum(carried_part.astype(jnp.bfloat16), "tp").astype(jnp.float32)
    stream_back = (stream_rows.astype(jnp.float32) + carried).astype(jnp.bfloat16)
    grad_one = (
        jnp.einsum("th,tc->hc", act_rows, stream_back, preferred_element_type=jnp.float32)
        * scale_hidden
    )
    weight = shard_counts[0, 0].astype(jnp.float32)
    total_one = lax.psum(weight, "row")
    total_two = lax.psum(weight, "col")
    term_one = rounded(weight * inner_rate * grad_one)
    term_two = rounded(weight * inner_rate * grad_two)
    share_one = COLS // n_rows
    share_two = COLS // n_cols
    whole_one = lax.psum(term_one.astype(jnp.bfloat16), "row").astype(jnp.float32)
    whole_two = lax.psum(term_two.astype(jnp.bfloat16), "col").astype(jnp.float32)
    sum_one = lax.dynamic_slice_in_dim(whole_one, row_index * share_one, share_one, 1)
    sum_two = lax.dynamic_slice_in_dim(whole_two, col_index * share_two, share_two, 1)
    out_one_new, out_one_moment_new = outer_step(
        first_store, out_one_moment[0], sum_one, total_one, share_one
    )
    in_two_new, in_two_moment_new = outer_step(
        second_store, in_two_moment[0], sum_two, total_two, share_two
    )
    return (out_one_new, out_one_moment_new, in_two_new, in_two_moment_new)


def solution(mesh):
    return jax.shard_map(
        on_device,
        mesh=mesh,
        in_specs=(
            P("row", "col", None, "tp"),
            P("row", "col", None, "tp"),
            P("row", "col", None, "tp"),
            P("row", "col", None, None),
            P("row", "col", None),
            P("row", "col"),
            P("col", "tp", "row"),
            P("row", "tp", "col"),
            P("col", "tp", "row"),
            P("row", "tp", "col"),
        ),
        out_specs=(
            P("col", "tp", "row"),
            P("col", "tp", "row"),
            P("row", "tp", "col"),
            P("row", "tp", "col"),
        ),
        check_vma=False,
    )
```

profile of v0, /device:TPU:1, one launch (start us, length us, event | category | flops | bytes accessed | tf_op | source)
XLA Modules:
  0.0 600.1 jit_solution(11245601122463545294)
XLA Ops:
  7.2 0.0 copy-start
  7.2 0.0 all-gather.9.cloned.1.call-start
  7.2 0.7 all-gather.9.cloned.1.call-update
  7.9 0.0 all-gather.11.cloned.1.call-start
  8.0 0.7 all-gather.11.cloned.1.call-update
  8.7 0.0 copy-start.7
  8.7 0.0 all-gather.7.cloned.1.call-start
  8.7 0.7 all-gather.7.cloned.1.call-update
  9.4 0.0 all-reduce.5.cloned.1.call-start
  9.5 67.7 %all-gather.9.cloned.1.call-done = bf16[1,1024,2048]{2,1,0:T(8,128)(2,1)} async-done(((bf16[1,1024,256]{2,1,0:T(8,128)(2,1)}), bf16[1,1024,2048]{2,1,0:T(8,128)(2,1)}) %all-gather.9.cloned.1.call-update) | async-done | bytes 4194320 | tf_op jit(solution)/shard_map/all_gather | solution.py:64
  77.1 0.0 copy-done
  77.1 4.4 fusion.7
  81.6 0.0 all-reduce.5.cloned.1.call-update
  81.6 0.0 all-reduce.7.cloned.1.call-start
  82.3 0.0 copy-done.7
  82.3 116.9 %all-gather.11.cloned.1.call-done = bf16[1,1024,2048]{2,1,0:T(8,128)(2,1)} async-done(((bf16[1,1024,256]{2,1,0:T(8,128)(2,1)}), bf16[1,1024,2048]{2,1,0:T(8,128)(2,1)}) %all-gather.11.cloned.1.call-update) | async-done | bytes 4194320 | tf_op jit(solution)/shard_map/all_gather | solution.py:72
  199.2 6.4 %copy.18 = bf16[1,1024,2048]{1,2,0:T(8,128)(2,1)} copy(bf16[1,1024,2048]{2,1,0:T(8,128)(2,1)} %all-gather.11.cloned.1.call-done) | data formatting | bytes 8388608 | tf_op jit(solution)/shard_map/all_gather | solution.py:72
  205.6 0.0 copy-start.6
  205.6 1.1 slice.17
  206.8 28.3 %all-gather.7.cloned.1.call-done = bf16[1,1,256,2048]{3,2,1,0:T(8,128)(2,1)} async-done(((bf16[1,1,256,256]{3,2,1,0:T(8,128)(2,1)}), bf16[1,1,256,2048]{3,2,1,0:T(8,128)(2,1)}) %all-gather.7.cloned.1.call-update) | async-done | bytes 1048592 | tf_op jit(solution)/shard_map/all_gather | solution.py:70
  235.0 79.2 %all-reduce.5.cloned.1.call-done = bf16[256,2048]{1,0:T(8,128)(2,1)} async-done(((bf16[256,2048]{1,0:T(8,128)(2,1)}), bf16[256,2048]{1,0:T(8,128)(2,1)}) %all-reduce.5.cloned.1.call-update) | async-done | bytes 1048592 | tf_op jit(solution)/shard_map/psum | solution.py:69
  314.3 1.9 fusion.10
  316.2 1.3 copy.23
  317.5 0.0 copy-done.6
  317.5 0.0 copy-start.3
  317.5 3.9 multiply_convert_fusion
  321.4 0.0 copy-start.1
  321.4 0.0 copy-start.2
  321.4 0.0 copy-start.4
  321.4 0.0 copy-start.5
  321.4 1.0 fusion.17
  322.4 0.0 all-reduce.7.cloned.1.call-update
  322.5 0.0 all-reduce.11.cloned.1.call-start
  322.5 0.9 slice.19
  323.4 1.2 fusion.15
  324.6 0.0 all-reduce.11.cloned.1.call-update
  324.6 0.0 all-reduce.9.cloned.1.call-start
  324.7 72.5 %all-reduce.7.cloned.1.call-done = bf16[256,256]{1,0:T(8,128)(2,1)} async-done(((bf16[256,256]{1,0:T(8,128)(2,1)}), bf16[256,256]{1,0:T(8,128)(2,1)}) %all-reduce.7.cloned.1.call-update) | async-done | bytes 131088 | tf_op jit(solution)/shard_map/psum | solution.py:91
  397.2 0.0 copy-done.3
  397.2 2.1 fusion.16
  399.3 0.0 all-reduce.9.cloned.1.call-update
  399.3 14.6 %psum.45 = f32[]{:T(128)} all-reduce(f32[]{:T(128)} %bitcast.9), channel_id=1, replica_groups=mesh['row'=8,'col'=8,'tp'=8] {'row'}, use_global_device_ids=true, to_apply=%region_3.4 | all-reduce | flops 1 | bytes 8 | tf_op jit(solution)/shard_map/psum | solution.py:98
  413.9 28.7 %psum.47 = f32[]{:T(128)} all-reduce(f32[]{:T(128)} %bitcast.9), channel_id=1, replica_groups=mesh['row'=8,'col'=8,'tp'=8] {'col'}, use_global_device_ids=true, to_apply=%region_5.6 | all-reduce | flops 1 | bytes 8 | tf_op jit(solution)/shard_map/psum | solution.py:99
  442.7 0.0 copy-done.1
  442.7 0.2 copy.17
  442.9 0.0 copy-done.2
  442.9 0.2 copy.19
  443.1 71.1 %all-reduce.11.cloned.1.call-done = bf16[1024,256]{0,1:T(8,128)(2,1)} async-done(((bf16[1024,256]{0,1:T(8,128)(2,1)}), bf16[1024,256]{0,1:T(8,128)(2,1)}) %all-reduce.11.cloned.1.call-update) | async-done | bytes 524304 | tf_op jit(solution)/shard_map/psum | solution.py:105
  514.2 0.0 copy-done.4
  514.2 2.2 fusion.24
  516.4 74.6 %all-reduce.9.cloned.1.call-done = bf16[1024,256]{0,1:T(8,128)(2,1)} async-done(((bf16[1024,256]{0,1:T(8,128)(2,1)}), bf16[1024,256]{0,1:T(8,128)(2,1)}) %all-reduce.9.cloned.1.call-update) | async-done | bytes 524304 | tf_op jit(solution)/shard_map/psum | solution.py:104
  591.0 0.0 copy-done.5
  591.0 2.3 fusion.23
  (1 shorter events, 0.0 us)
Async XLA Ops:
  7.2 69.9 %copy-start = (bf16[1,1,256,1024]{3,2,1,0:T(8,128)(2,1)S(1)}, bf16[1,1,256,1024]{3,2,1,0:T(8,128)(2,1)}, u32[]{:S(2)}) copy-start(bf16[1,1,256,1024]{3,2,1,0:T(8,128)(2,1)} %param.10) | copy-start | bytes 1572868
  7.2 69.9 %all-gather.9.cloned.1.call-start = ((), (), s32[]{:S(2)}) async-start(), calls=%async_computation.5 | async-start | bytes 4718592 | tf_op jit(solution)/shard_map/all_gather | solution.py:64
  7.9 191.3 %all-gather.11.cloned.1.call-start = ((), (), s32[]{:S(2)}) async-start(), calls=%async_computation.6 | async-start | bytes 4718592 | tf_op jit(solution)/shard_map/all_gather | solution.py:72
  8.7 73.6 %copy-start.7 = (s32[1,1,256]{2,1,0:T(1,128)S(1)}, s32[1,1,256]{2,1,0:T(1,128)}, u32[]{:S(2)}) copy-start(s32[1,1,256]{2,1,0:T(1,128)} %param.14) | copy-start | bytes 3076
  8.7 226.4 %all-gather.7.cloned.1.call-start = ((), (), s32[]{:S(2)}) async-start(), calls=%async_computation.4 | async-start | bytes 1179648 | tf_op jit(solution)/shard_map/all_gather | solution.py:70
  9.4 304.9 %all-reduce.5.cloned.1.call-start = ((), (), s32[]{:S(2)}) async-start(), calls=%async_computation | async-start | bytes 2097152 | tf_op jit(solution)/shard_map/psum | solution.py:69
  81.6 315.6 %all-reduce.7.cloned.1.call-start = ((), (), s32[]{:S(2)}) async-start(), calls=%async_computation.1 | async-start | bytes 262144 | tf_op jit(solution)/shard_map/psum | solution.py:91
  205.6 111.9 %copy-start.6 = (bf16[1,1,256,1024]{3,2,1,0:T(8,128)(2,1)S(1)}, bf16[1,1,256,1024]{3,2,1,0:T(8,128)(2,1)}, u32[]{:S(2)}) copy-start(bf16[1,1,256,1024]{3,2,1,0:T(8,128)(2,1)} %param.12) | copy-start | bytes 1572868
  317.5 79.7 %copy-start.3 = (bf16[1,1,256,256]{3,2,1,0:T(8,128)(2,1)S(1)}, bf16[1,1,256,256]{3,2,1,0:T(8,128)(2,1)}, u32[]{:S(2)}) copy-start(bf16[1,1,256,256]{3,2,1,0:T(8,128)(2,1)} %param.13) | copy-start | bytes 393220
  321.4 121.3 %copy-start.1 = (bf16[1,1024,256]{2,1,0:T(8,128)(2,1)S(1)}, bf16[1,1024,256]{2,1,0:T(8,128)(2,1)}, u32[]{:S(2)}) copy-start(bf16[1,1024,256]{2,1,0:T(8,128)(2,1)} %param.16) | copy-start | bytes 1572868
  321.4 121.5 %copy-start.2 = (bf16[1,1024,256]{2,1,0:T(8,128)(2,1)S(1)}, bf16[1,1024,256]{2,1,0:T(8,128)(2,1)}, u32[]{:S(2)}) copy-start(bf16[1,1024,256]{2,1,0:T(8,128)(2,1)} %param.17) | copy-start | bytes 1572868
  321.4 192.8 %copy-start.4 = (f32[1,1024,32]{1,2,0:T(8,128)S(1)}, f32[1,1024,32]{1,2,0:T(8,128)}, u32[]{:S(2)}) copy-start(f32[1,1024,32]{1,2,0:T(8,128)} %param.19) | copy-start | bytes 393220
  321.4 269.5 %copy-start.5 = (f32[1,1024,32]{1,2,0:T(8,128)S(1)}, f32[1,1024,32]{1,2,0:T(8,128)}, u32[]{:S(2)}) copy-start(f32[1,1024,32]{1,2,0:T(8,128)} %param.18) | copy-start | bytes 393220
  322.5 191.7 %all-reduce.11.cloned.1.call-start = ((), (), s32[]{:S(2)}) async-start(), calls=%async_computation.3 | async-start | bytes 1048576 | tf_op jit(solution)/shard_map/psum | solution.py:105
  324.6 266.4 %all-reduce.9.cloned.1.call-start = ((), (), s32[]{:S(2)}) async-start(), calls=%async_computation.2 | async-start | bytes 1048576 | tf_op jit(solution)/shard_map/psum | solution.py:104
Sparse Core Ops, SparseCore 0:
  10.0 67.0 all-gather.8
  80.2 118.9 all-gather.10
  201.2 33.8 all-gather.6
  237.8 76.3 all-reduce.4
  322.6 74.5 all-reduce.6
  400.2 113.9 all-reduce.10
  516.5 74.4 all-reduce.8
where the time goes:
time: 605 us; the launch traced here: 600 us
  waiting for transfers between devices  512 us (85%)
  blocking collectives  43.4 us (7%)
  between operations  14.9 us (2%)
  matrix products  12.6 us (2%)
  local copies, waits for them, and re-layouts  10.3 us (2%)
  other arithmetic  6.43 us (1%)
    all_gather x1, waiting for transfers between devices, on_device(): second_weight = lax.all_gather(second_store, 'col', axis=1, tiled=True)  117 us
    psum x1, waiting for transfers between devices, on_device(): lax.psum(partial_value.astype(jnp.bfloat16), 'tp').astype(jnp.float32)  79.2 us
    psum x1, waiting for transfers between devices, on_device(): lax.psum(term_one.astype(jnp.bfloat16), 'row').astype(jnp.float32)  74.6 us
    psum x1, waiting for transfers between devices, on_device(): lax.psum(carried_part.astype(jnp.bfloat16), 'tp').astype(jnp.float32)  72.5 us
    psum x1, waiting for transfers between devices, on_device(): lax.psum(term_two.astype(jnp.bfloat16), 'col').astype(jnp.float32)  71.1 us
    all_gather x1, waiting for transfers between devices, on_device(): lax.all_gather(first_store, 'row', axis=1, tiled=True)  67.7 us
    psum x1, blocking collectives, on_device(): total_two = lax.psum(weight, 'col')  28.7 us
    all_gather x1, waiting for transfers between devices, on_device(): resid_all = lax.all_gather(resid_rows, 'tp', axis=1, tiled=True)  28.3 us
  transfers between devices with their start and end apart: 7, of which 7 were waited for; matrix products, arithmetic and copies ran while one was open for 3% of the time, Pallas kernels for 0%

commit v1 on v0

v1 whole, which is shorter than its diff:
```python
import math

import jax
import jax.numpy as jnp
from jax import lax
from jax.experimental import pallas as pl
from jax.experimental.pallas import tpu as pltpu
from jax.sharding import PartitionSpec as P

D = 2048
H = 8192
TOK = 256
HID = 1024
BLK = 256
SEL = 32
INNER = 4.0
OUTER = 0.7
DECAY = 0.9
MESH = pl.DeviceIdType.MESH
BF = jnp.bfloat16
F32 = jnp.float32

SCALE_MODEL = 1.0 / math.sqrt(D)
SCALE_HIDDEN = 1.0 / math.sqrt(H)
NT = (((1,), (1,)), ((), ()))
OFFSETS = (0, 7, 1, 6, 2, 5, 3, 4)


def kernel(
    act_h, res_h, up_h, st_h, ids_h, cnt_v, w1_h, w2_h, m1_h, m2_h,
    o1, n1, o2, n2,
    act, res, up, st, ids, w1g, w2g, m1, m2,
    part, cin, zb, zin, y, relay, pre2, slope, selw, sely, stt, pc1, pc2,
    q, qin, dy, t1, t1in, t2, t2x, t2z, t2zin, wown, wrow, wcol,
    loc, w1s, w1r, w2s, w2r, zs, zr,
    crs, crr, zrs, zrr, ags, agr, cgs, cgr,
    qs, qr, ds_, dr_, rs_, rr_, xs, xr, as_, ar_, nrs, nrr, ncs, ncr,
):
    r = lax.axis_index("row")
    c = lax.axis_index("col")
    t = lax.axis_index("tp")
    x = lax.div(c, 2)
    zh = lax.rem(c, 2)
    zl = lax.div(t, 2)
    core = lax.rem(t, 2)
    z = zh * 4 + zl
    other = (r, c, zl * 2 + 1 - core)

    def row_dev(d):
        return (lax.rem(r + d, 8), c, t)

    def tp_dev(d):
        return (r, c, lax.rem(t + d, 8))

    def x_dev(d):
        return (r, lax.rem(x + d, 4) * 2 + zh, t)

    def z_dev(d):
        to = lax.rem(z + d, 8)
        return (r, x * 2 + lax.div(to, 4), lax.rem(to, 4) * 2 + core)

    def zl_dev(d):
        return (r, c, lax.rem(zl + d, 4) * 2 + core)

    def col_dev(d):
        return (r, lax.rem(c + d, 8), t)

    antipode = (r, x * 2 + 1 - zh, t)
    pending = []

    def send(src, dst, s_sem, r_sem, device):
        copy = pltpu.make_async_remote_copy(
            src_ref=src, dst_ref=dst, send_sem=s_sem, recv_sem=r_sem,
            device_id=device, device_id_type=MESH,
        )
        copy.start()
        pending.append(copy)

    def arrive(dst, s_sem, r_sem):
        pltpu.make_async_remote_copy(
            src_ref=dst, dst_ref=dst, send_sem=s_sem, recv_sem=r_sem,
            device_id=other, device_id_type=MESH,
        ).wait_recv()

    local = [
        pltpu.make_async_copy(a, b, loc.at[k])
        for k, (a, b) in enumerate(
            (
                (w1_h, w1g.at[r]), (w2_h, w2g.at[c]), (act_h, act), (res_h, res),
                (up_h, up), (st_h, st), (ids_h, ids), (m1_h, m1), (m2_h, m2),
            )
        )
    ]
    for copy in local:
        copy.start()

    barrier = pltpu.get_barrier_semaphore()
    partners = (
        [row_dev(d) for d in range(1, 8)]
        + [col_dev(d) for d in range(1, 8)]
        + [tp_dev(d) for d in range(1, 8)]
        + [z_dev(2), z_dev(6)]
    )
    for device in partners:
        pl.semaphore_signal(barrier, inc=1, device_id=device, device_id_type=MESH)
    weight = cnt_v[...].astype(F32)
    wown[...] = jnp.broadcast_to(weight, (8, 128))
    pl.semaphore_wait(barrier, len(partners))

    def w1_chunk(n, half):
        return w1g.at[n, pl.ds(512 * half, 512)]

    def w1_send(way, step, j):
        n = lax.rem(r + (8 - step if way == 0 else step), 8)
        half = j if way == 0 else 1 - j
        ref = w1_chunk(n, half)
        send(ref, ref, w1s.at[way, step, j], w1r.at[way, step, j], row_dev(1 if way == 0 else 7))

    def w1_wait(way, step, j):
        n = lax.rem(r + (7 - step if way == 0 else step + 1), 8)
        half = j if way == 0 else 1 - j
        arrive(w1_chunk(n, half), w1s.at[way, step, j], w1r.at[way, step, j])

    def w2_chunk(at, phase, half):
        plane = zh if phase == 0 else 1 - zh
        return w2g.at[lax.rem(at, 4) * 2 + plane, pl.ds(512 * half, 512)]

    def w2_send(phase, way, j):
        half = j % 2 if way == 0 else 1 - j % 2
        back = 0 if j < 2 else 1
        at = x + (4 - back if way == 0 else back)
        ref = w2_chunk(at, phase, half)
        send(ref, ref, w2s.at[phase, way, j], w2r.at[phase, way, j], x_dev(1 if way == 0 else 3))

    def w2_wait(phase, way, j):
        half = j % 2 if way == 0 else 1 - j % 2
        back = 1 if j < 2 else 2
        at = x + (4 - back if way == 0 else back)
        arrive(w2_chunk(at, phase, half), w2s.at[phase, way, j], w2r.at[phase, way, j])

    def z_first(way):
        send(
            w2g.at[c, pl.ds(512 * way, 512)], relay.at[way],
            zs.at[way, 0], zr.at[way, 0], z_dev(2 if way == 0 else 6),
        )

    def z_second(way):
        arrive(relay.at[way], zs.at[way, 0], zr.at[way, 0])
        hop = 2 if way == 0 else 6
        far = lax.div(lax.rem(z + hop, 8), 4)
        send(
            relay.at[way], w2g.at[x * 2 + 1 - far, pl.ds(512 * way, 512)],
            zs.at[way, 1], zr.at[way, 1], z_dev(hop),
        )

    def z_wait(way):
        arrive(w2g.at[x * 2 + 1 - zh, pl.ds(512 * way, 512)], zs.at[way, 1], zr.at[way, 1])

    local[0].wait()
    for j in range(2):
        for way in range(2):
            w1_send(way, 0, j)
    local[1].wait()
    for j in range(2):
        for way in range(2):
            w2_send(0, way, j)
    for way in range(2):
        z_first(way)
    for d in range(1, 8):
        send(wown, wrow.at[d - 1], nrs.at[d - 1], nrr.at[d - 1], row_dev(d))
        send(wown, wcol.at[d - 1], ncs.at[d - 1], ncr.at[d - 1], col_dev(d))
    for copy in local[2:]:
        copy.wait()

    def block(i):
        return lax.rem(r + OFFSETS[i], 8)

    def stage0(i):
        n = block(i)
        acc = jnp.dot(act[...], w1g[n], preferred_element_type=F32) * SCALE_HIDDEN
        mine = jnp.where(n == t, 1.0, 0.0).astype(F32)
        acc = acc + res[...].astype(F32) * mine
        part[i] = acc.astype(BF).reshape(2, 128, BLK)
        send(part.at[i, 1 - core], cin.at[i], crs.at[i], crr.at[i], other)

    def stage1(i):
        arrive(cin.at[i], crs.at[i], crr.at[i])
        both = part[i, core].astype(F32) + cin[i].astype(F32)
        zb[i] = both.astype(BF).reshape(4, SEL, BLK)
        for d in range(1, 4):
            send(
                zb.at[i, lax.rem(zl + d, 4)], zin.at[i, d - 1],
                zrs.at[i, d - 1], zrr.at[i, d - 1], zl_dev(d),
            )

    def stage2(i):
        n = block(i)
        total = zb[i, zl].astype(F32)
        for d in range(1, 4):
            arrive(zin.at[i, d - 1], zrs.at[i, d - 1], zrr.at[i, d - 1])
            total = total + zin[i, d - 1].astype(F32)
        y[n, core, zl] = total.astype(BF)
        for d in range(1, 4):
            ref = y.at[n, core, zl]
            send(ref, ref, ags.at[i, d - 1], agr.at[i, d - 1], zl_dev(d))

    def stage3(i):
        n = block(i)
        for d in range(1, 4):
            arrive(y.at[n, core, lax.rem(zl + 4 - d, 4)], ags.at[i, d - 1], agr.at[i, d - 1])
        ref = y.at[n, core]
        send(ref, ref, cgs.at[i], cgr.at[i], other)

    def stage4(i):
        n = block(i)
        arrive(y.at[n, 1 - core], cgs.at[i], cgr.at[i])

    def y_block(i):
        return y[block(i)].reshape(TOK, BLK)

    first_rows = (
        lax.broadcasted_iota(jnp.int32, (SEL, BLK), 0)
        == lax.broadcasted_iota(jnp.int32, (SEL, BLK), 1)
    ).astype(F32).astype(BF)

    def pick_y(i):
        n = block(i)
        sely[n] = lax.dot_general(first_rows, y_block(i), NT, preferred_element_type=F32).astype(BF)

    def forward(blocks):
        total = None
        for i in blocks:
            n = block(i)
            term = lax.dot_general(y_block(i), w2g[n], NT, preferred_element_type=F32)
            total = term if total is None else total + term
        return total

    def prepare():
        keep_row = (ids[...] != 0).astype(F32)
        across = lax.broadcasted_iota(jnp.int32, (TOK, TOK), 0)
        along = lax.broadcasted_iota(jnp.int32, (TOK, TOK), 1)
        keep_col = jnp.sum(
            jnp.where(across == along, jnp.broadcast_to(keep_row, (TOK, TOK)), 0.0),
            axis=1, keepdims=True,
        )
        up[...] = (up[...].astype(F32) * keep_col).astype(BF)
        own_rows = (
            lax.broadcasted_iota(jnp.int32, (SEL, BLK), 0) + SEL * t
            == lax.broadcasted_iota(jnp.int32, (SEL, BLK), 1)
        ).astype(F32).astype(BF)
        stt[...] = lax.dot_general(own_rows, st[...], NT, preferred_element_type=F32) * keep_row
        pc1[...] = lax.dot_general(first_rows, w1g[r], NT, preferred_element_type=F32)
        pc2[...] = lax.dot_general(first_rows, w2g[c], NT, preferred_element_type=F32)

    stage0(0)
    prepare()
    stage1(0)
    stage2(0)
    for way in range(2):
        w1_wait(way, 0, 0)
        w1_send(way, 1, 0)
    for way in range(2):
        w2_wait(0, way, 0)
        w2_send(0, way, 2)
    stage3(0)
    for way in range(2):
        w1_wait(way, 0, 1)
        w1_send(way, 1, 1)
    stage0(1)
    stage0(2)
    for way in range(2):
        z_second(way)
    stage4(0)
    pick_y(0)
    stage1(1)
    stage1(2)
    for way in range(2):
        w2_wait(0, way, 1)
    for way in range(2):
        w1_wait(way, 1, 0)
        w1_send(way, 2, 0)
    stage2(1)
    stage2(2)
    for way in range(2):
        w2_wait(0, way, 2)
    stage3(1)
    stage3(2)
    for way in range(2):
        w1_wait(way, 1, 1)
        w1_send(way, 2, 1)
    stage0(3)
    stage0(4)
    stage4(1)
    stage4(2)
    pick_y(1)
    pick_y(2)
    stage1(3)
    stage1(4)
    for way in range(2):
        z_wait(way)
    for j in range(2):
        for way in range(2):
            w2_send(1, way, j)
    for way in range(2):
        w1_wait(way, 2, 0)
        w1_send(way, 3, 0)
    stage2(3)
    stage2(4)
    stage3(3)
    stage3(4)
    for way in range(2):
        w2_wait(1, way, 0)
        w2_send(1, way, 2)
    for way in range(2):
        w1_wait(way, 2, 1)
    stage0(5)
    stage0(6)
    stage4(3)
    stage4(4)
    pick_y(3)
    pick_y(4)
    stage1(5)
    stage1(6)
    for way in range(2):
        w1_wait(way, 3, 0)
    stage0(7)
    stage2(5)
    stage2(6)
    stage1(7)
    stage3(5)
    stage3(6)
    stage2(7)
    stage4(5)
    stage4(6)
    pick_y(5)
    pick_y(6)
    for way in range(2):
        w2_wait(1, way, 1)
    for way in range(2):
        w2_wait(1, way, 2)
    for n in range(8):
        selw[n] = lax.dot_general(first_rows, w2g[n], NT, preferred_element_type=F32).astype(BF)
    stage3(7)
    pre2[...] = forward(range(7))
    stage4(7)
    pick_y(7)

    last = block(7)
    y_last = y_block(7)
    carried = jnp.zeros((BLK, TOK), F32)
    for k in range(4):
        cols = slice(256 * k, 256 * k + 256)
        pre = pre2[:, cols] + lax.dot_general(
            y_last, w2g[last, cols], NT, preferred_element_type=F32
        )
        pre = pre * SCALE_MODEL
        squash = jax.nn.sigmoid(pre)
        piece = (up[:, cols].astype(F32) * squash * (1.0 + pre * (1.0 - squash))).astype(BF)
        slope[:, cols] = piece
        carried = carried + lax.dot_general(
            selw[:, :, cols].reshape(BLK, 256), piece, NT, preferred_element_type=F32
        )
    q[...] = (carried * SCALE_MODEL).astype(BF).reshape(8, SEL, TOK)
    for d in range(1, 8):
        send(q.at[lax.rem(t + d, 8)], qin.at[d - 1], qs.at[d - 1], qr.at[d - 1], tp_dev(d))

    factor = weight * INNER
    grad = jnp.dot(sely[...].reshape(BLK, TOK), slope[...], preferred_element_type=F32) * SCALE_MODEL
    t2[...] = (factor * grad).astype(BF).reshape(4, 2, SEL, HID)
    for d in range(1, 4):
        send(t2.at[lax.rem(x + d, 4)], t2x.at[d - 1], xs.at[d - 1], xr.at[d - 1], x_dev(d))

    total = q[t].astype(F32) + stt[...]
    for d in range(1, 8):
        arrive(qin.at[d - 1], qs.at[d - 1], qr.at[d - 1])
        total = total + qin[d - 1].astype(F32)
    dy[t] = total.astype(BF)
    for d in range(1, 8):
        ref = dy.at[t]
        send(ref, ref, ds_.at[d - 1], dr_.at[d - 1], tp_dev(d))
    for d in range(1, 8):
        arrive(dy.at[lax.rem(t + 8 - d, 8)], ds_.at[d - 1], dr_.at[d - 1])
    grad = jnp.dot(dy[...].reshape(BLK, TOK), act[...], preferred_element_type=F32) * SCALE_HIDDEN
    t1[...] = (factor * grad).astype(BF).reshape(8, SEL, HID)
    for d in (4, 3, 5, 2, 6, 1, 7):
        send(t1.at[lax.rem(r + d, 8)], t1in.at[d - 1], rs_.at[d - 1], rr_.at[d - 1], row_dev(d))

    far = t2[x, 1 - zh].astype(F32)
    near = t2[x, zh].astype(F32)
    for d in range(1, 4):
        arrive(t2x.at[d - 1], xs.at[d - 1], xr.at[d - 1])
        far = far + t2x[d - 1, 1 - zh].astype(F32)
        near = near + t2x[d - 1, zh].astype(F32)
    t2z[...] = far.astype(BF)
    send(t2z, t2zin, as_, ar_, antipode)

    def total_of(buffer, s_sems, r_sems):
        count = wown[...]
        for d in range(1, 8):
            arrive(buffer.at[d - 1], s_sems.at[d - 1], r_sems.at[d - 1])
            count = count + buffer[d - 1]
        return count[0:1, 0:1]

    total_one = total_of(wrow, nrs, nrr)
    total_two = total_of(wcol, ncs, ncr)

    arrive(t2zin, as_, ar_)
    delta = (near + t2zin[...].astype(F32)) / total_two
    moment = DECAY * m2[...] + delta
    n2[...] = moment
    o2[...] = pc2[...] - OUTER * (delta + DECAY * moment)

    summed = t1[r].astype(F32)
    for d in (1, 7, 2, 6, 3, 5, 4):
        arrive(t1in.at[d - 1], rs_.at[d - 1], rr_.at[d - 1])
        summed = summed + t1in[d - 1].astype(F32)
    delta = summed / total_one
    moment = DECAY * m1[...] + delta
    n1[...] = moment
    o1[...] = pc1[...] - OUTER * (delta + DECAY * moment)

    for copy in pending:
        copy.wait_send()


def on_device(
    act_one, residual, upstream, stream_grad, token_ids, shard_counts,
    out_one, in_two, out_one_moment, in_two_moment,
):
    dma = pltpu.SemaphoreType.DMA
    vmem = pltpu.VMEM
    whole = pl.BlockSpec(memory_space=pl.ANY)
    inside = pl.BlockSpec(memory_space=pltpu.VMEM)
    scratch = [
        vmem((TOK, HID), BF), vmem((TOK, BLK), BF), vmem((TOK, HID), BF), vmem((TOK, BLK), BF),
        vmem((1, TOK), jnp.int32), vmem((8, HID, BLK), BF), vmem((8, HID, BLK), BF),
        vmem((SEL, HID), F32), vmem((SEL, HID), F32),
        vmem((8, 2, 128, BLK), BF), vmem((8, 128, BLK), BF),
        vmem((8, 4, SEL, BLK), BF), vmem((8, 3, SEL, BLK), BF),
        vmem((8, 2, 4, SEL, BLK), BF), vmem((2, 512, BLK), BF),
        vmem((TOK, HID), F32), vmem((TOK, HID), BF), vmem((8, SEL, HID), BF),
        vmem((8, SEL, TOK), BF), vmem((SEL, TOK), F32), vmem((SEL, HID), F32), vmem((SEL, HID), F32),
        vmem((8, SEL, TOK), BF), vmem((7, SEL, TOK), BF), vmem((8, SEL, TOK), BF),
        vmem((8, SEL, HID), BF), vmem((7, SEL, HID), BF),
        vmem((4, 2, SEL, HID), BF), vmem((3, 2, SEL, HID), BF),
        vmem((SEL, HID), BF), vmem((SEL, HID), BF),
        vmem((8, 128), F32), vmem((7, 8, 128), F32), vmem((7, 8, 128), F32),
        dma((9,)),
        dma((2, 4, 2)), dma((2, 4, 2)), dma((2, 2, 3)), dma((2, 2, 3)), dma((2, 2)), dma((2, 2)),
        dma((8,)), dma((8,)), dma((8, 3)), dma((8, 3)), dma((8, 3)), dma((8, 3)), dma((8,)), dma((8,)),
        dma((7,)), dma((7,)), dma((7,)), dma((7,)), dma((7,)), dma((7,)),
        dma((3,)), dma((3,)), dma(()), dma(()), dma((7,)), dma((7,)), dma((7,)), dma((7,)),
    ]
    result = jax.ShapeDtypeStruct((SEL, HID), F32)
    o1, n1, o2, n2 = pl.pallas_call(
        kernel,
        out_shape=(result,) * 4,
        in_specs=[whole] * 5 + [inside] + [whole] * 4,
        out_specs=(inside,) * 4,
        scratch_shapes=scratch,
        compiler_params=pltpu.CompilerParams(
            collective_id=0, has_side_effects=True, vmem_limit_bytes=48 * 1024 * 1024
        ),
        cost_estimate=pl.CostEstimate(flops=3_000_000_000, bytes_accessed=4_000_000, transcendentals=300_000),
    )(
        act_one[0, 0], residual[0, 0], upstream[0, 0], stream_grad[0, 0], token_ids[0],
        shard_counts, out_one[0], in_two[0], out_one_moment[0].T, in_two_moment[0].T,
    )
    return (o1.T[None], n1.T[None], o2.T[None], n2.T[None])


def solution(mesh):
    return jax.shard_map(
        on_device,
        mesh=mesh,
        in_specs=(
            P("row", "col", None, "tp"),
            P("row", "col", None, "tp"),
            P("row", "col", None, "tp"),
            P("row", "col", None, None),
            P("row", "col", None),
            P("row", "col"),
            P("col", "tp", "row"),
            P("row", "tp", "col"),
            P("col", "tp", "row"),
            P("row", "tp", "col"),
        ),
        out_specs=(
            P("col", "tp", "row"),
            P("col", "tp", "row"),
            P("row", "tp", "col"),
            P("row", "tp", "col"),
        ),
        check_vma=False,
    )
```

time: 605 us -> 121 us (0.20)
  waiting for transfers between devices: 512 us -> 0 us
  Pallas kernels: 0 us -> 109 us
  blocking collectives: 43.4 us -> 0 us
  between operations: 14.9 us -> 1.31 us
  matrix products: 12.6 us -> 0 us
  other arithmetic: 6.43 us -> 0 us
    psum x4 -> x0, waiting for transfers between devices: 297 us -> none  [the longest x1 79.2 us: on_device(): lax.psum(partial_value.astype(jnp.bfloat16), 'tp').astype(jnp.float32)]
    all_gather x3 -> x0, waiting for transfers between devices: 213 us -> none  [the longest x1 117 us: on_device(): second_weight = lax.all_gather(second_store, 'col', axis=1, tiled=True)]
    pallas_call x0 -> x1, Pallas kernels: none -> 109 us  [on_device(): pl.pallas_call(kernel, out_shape=(result,) * 4, in_specs=[whole] * 5 + [i...]
    psum x2 -> x0, blocking collectives: 43.4 us -> none  [the longest x1 28.7 us: on_device(): total_two = lax.psum(weight, 'col')]
    dot_general x5 -> x0, matrix products: 12.6 us -> none  [the longest x1 4.44 us: on_device(): jnp.dot(act_rows, lax.all_gather(first_store, 'row', axis=1, tiled=True),...]
    unnamed x18 -> x22, local copies, waits for them, and re-layouts: 0.46 us -> 11.1 us
    all_gather x1 -> x0, local copies, waits for them, and re-layouts: 6.43 us -> none  [on_device(): second_weight = lax.all_gather(second_store, 'col', axis=1, tiled=True)]
  transfers between devices with their start and end apart: 7 -> 0, of which waited for: 7 -> 0; matrix products, arithmetic and copies ran while one was open for 3% -> 0% of each run, Pallas kernels for 0% -> 0%
where the time goes in v1:
time: 121 us
  Pallas kernels  109 us (90%)
  local copies, waits for them, and re-layouts  11.1 us (9%)
  between operations  1.31 us (1%)
    pallas_call x1, Pallas kernels, on_device(): pl.pallas_call(kernel, out_shape=(result,) * 4, in_specs=[whole] * 5 + [i...  109 us
    unnamed x22, local copies, waits for them, and re-layouts  11.1 us

profile of v1, /device:TPU:1, one launch (start us, length us, event | category | flops | bytes accessed | tf_op | source)
XLA Modules:
  0.0 121.0 jit_solution(4315697077582233600)
XLA Ops:
  1.3 0.0 copy-start.8
  1.3 0.7 copy-done.8
  2.0 0.0 copy-start
  2.0 1.0 copy-done
  3.0 0.0 copy-start.1
  3.0 1.0 copy-done.1
  4.0 0.0 copy-start.2
  4.0 1.0 copy-done.2
  5.1 0.0 copy-start.3
  5.1 1.0 copy-done.3
  6.1 0.0 copy-start.4
  6.1 0.9 copy-done.4
  7.0 0.0 copy-start.5
  7.0 0.9 copy-done.5
  7.9 0.0 copy-start.6
  7.9 0.9 copy-done.6
  8.8 0.0 copy-start.7
  8.8 0.9 copy-done.7
  9.7 108.7 %shard_map.129 = (f32[32,1024]{1,0:T(8,128)S(1)}, f32[32,1024]{1,0:T(8,128)S(1)}, f32[32,1024]{1,0:T(8,128)S(1)}, f32[32,1024]{1,0:T(8,128)S(1)}) custom-call(bf16[256,1024]{1,0:T(8,128)(2,1)S(1)} %bitcast.29, bf16[256,256]{1,0:T(8,128)(2,1)S(1)} %bitcast.33, bf16[256,1024]{1,0:T(8,128)(2,1)S(1)} %bitcast.30, bf16[256,256]{1,0:T(8,128)(2,1)S(1)} %bitcast.34, ...), custom_call_target="tpu_custom_call" | custom-call | flops 3000000000 | bytes 4000000 | tf_op jit(solution)/shard_map/pallas_call | solution.py:455
  118.4 0.7 copy.19
  119.1 0.7 copy.20
  119.7 0.7 copy.21
  120.4 0.7 copy.22
Async XLA Ops:
  1.3 0.7 copy-start.8
  2.0 1.0 copy-start
  3.0 1.0 copy-start.1
  4.0 1.0 copy-start.2
  5.1 1.0 copy-start.3
  6.1 0.9 copy-start.4
  7.0 0.9 copy-start.5
  7.9 0.9 copy-start.6
  8.8 0.9 copy-start.7

commit v2 on v1

--- a/solution.py
+++ b/solution.py
@@ -23,7 +23,7 @@
 SCALE_MODEL = 1.0 / math.sqrt(D)
 SCALE_HIDDEN = 1.0 / math.sqrt(H)
 NT = (((1,), (1,)), ((), ()))
-OFFSETS = (0, 7, 1, 6, 2, 5, 3, 4)
+HALF = 128
 
 
 def kernel(
@@ -86,7 +86,8 @@
         pltpu.make_async_copy(a, b, loc.at[k])
         for k, (a, b) in enumerate(
             (
-                (w1_h, w1g.at[r]), (w2_h, w2g.at[c]), (act_h, act), (res_h, res),
+                (w1_h.at[:, pl.ds(0, HALF)], w1g.at[r, 0]), (w1_h.at[:, pl.ds(HALF, HALF)], w1g.at[r, 1]),
+                (w2_h, w2g.at[c]), (act_h, act), (res_h, res),
                 (up_h, up), (st_h, st), (ids_h, ids), (m1_h, m1), (m2_h, m2),
             )
         )
@@ -107,19 +108,19 @@
     wown[...] = jnp.broadcast_to(weight, (8, 128))
     pl.semaphore_wait(barrier, len(partners))
 
-    def w1_chunk(n, half):
-        return w1g.at[n, pl.ds(512 * half, 512)]
+    def chunk(way, step, j):
+        return lax.rem(r + (8 - step if way == 0 else step), 8), (j if way == 0 else 1 - j)
 
     def w1_send(way, step, j):
-        n = lax.rem(r + (8 - step if way == 0 else step), 8)
-        half = j if way == 0 else 1 - j
-        ref = w1_chunk(n, half)
+        ref = w1g.at[chunk(way, step, j)]
         send(ref, ref, w1s.at[way, step, j], w1r.at[way, step, j], row_dev(1 if way == 0 else 7))
 
-    def w1_wait(way, step, j):
-        n = lax.rem(r + (7 - step if way == 0 else step + 1), 8)
-        half = j if way == 0 else 1 - j
-        arrive(w1_chunk(n, half), w1s.at[way, step, j], w1r.at[way, step, j])
+    def ring(k):
+        step, j = divmod(k - 1, 2)
+        for way in range(2):
+            arrive(w1g.at[chunk(way, step + 1, j)], w1s.at[way, step, j], w1r.at[way, step, j])
+            if step < 2 or (step == 2 and j == 0):
+                w1_send(way, step + 1, j)
 
     def w2_chunk(at, phase, half):
         plane = zh if phase == 0 else 1 - zh
@@ -157,31 +158,41 @@
         arrive(w2g.at[x * 2 + 1 - zh, pl.ds(512 * way, 512)], zs.at[way, 1], zr.at[way, 1])
 
     local[0].wait()
+    local[1].wait()
     for j in range(2):
         for way in range(2):
             w1_send(way, 0, j)
-    local[1].wait()
+    local[2].wait()
     for j in range(2):
         for way in range(2):
             w2_send(0, way, j)
     for way in range(2):
         z_first(way)
-    for d in range(1, 8):
-        send(wown, wrow.at[d - 1], nrs.at[d - 1], nrr.at[d - 1], row_dev(d))
-        send(wown, wcol.at[d - 1], ncs.at[d - 1], ncr.at[d - 1], col_dev(d))
-    for copy in local[2:]:
+    for copy in local[3:]:
         copy.wait()
 
-    def block(i):
-        return lax.rem(r + OFFSETS[i], 8)
-
-    def stage0(i):
-        n = block(i)
-        acc = jnp.dot(act[...], w1g[n], preferred_element_type=F32) * SCALE_HIDDEN
-        mine = jnp.where(n == t, 1.0, 0.0).astype(F32)
-        acc = acc + res[...].astype(F32) * mine
-        part[i] = acc.astype(BF).reshape(2, 128, BLK)
-        send(part.at[i, 1 - core], cin.at[i], crs.at[i], crr.at[i], other)
+    def send_counts():
+        for d in range(1, 8):
+            send(wown, wrow.at[d - 1], nrs.at[d - 1], nrr.at[d - 1], row_dev(d))
+            send(wown, wcol.at[d - 1], ncs.at[d - 1], ncr.at[d - 1], col_dev(d))
+
+    def group(g):
+        step, j = (0, 0) if g == 0 else ((g + 1) // 2, (g - 1) % 2)
+        first = chunk(0, step, j)
+        second = chunk(1, step, j)
+        return first, second
+
+    def stage0(g):
+        (na, ha), (nb, hb) = group(g)
+        rhs = jnp.concatenate([w1g[na, ha], w1g[nb, hb]], axis=1)
+        acc = jnp.dot(act[...], rhs, preferred_element_type=F32) * SCALE_HIDDEN
+        own = []
+        for n, half in ((na, ha), (nb, hb)):
+            mine = jnp.where(n == t, 1.0, 0.0).astype(F32)
+            own.append(res[:, HALF * half : HALF * half + HALF].astype(F32) * mine)
+        acc = acc + jnp.concatenate(own, axis=1)
+        part[g] = acc.astype(BF).reshape(2, 128, BLK)
+        send(part.at[g, 1 - core], cin.at[g], crs.at[g], crr.at[g], other)
 
     def stage1(i):
         arrive(cin.at[i], crs.at[i], crr.at[i])
@@ -194,46 +205,60 @@
             )
 
     def stage2(i):
-        n = block(i)
         total = zb[i, zl].astype(F32)
         for d in range(1, 4):
             arrive(zin.at[i, d - 1], zrs.at[i, d - 1], zrr.at[i, d - 1])
             total = total + zin[i, d - 1].astype(F32)
-        y[n, core, zl] = total.astype(BF)
+        y[i, core, zl] = total.astype(BF)
         for d in range(1, 4):
-            ref = y.at[n, core, zl]
+            ref = y.at[i, core, zl]
             send(ref, ref, ags.at[i, d - 1], agr.at[i, d - 1], zl_dev(d))
 
     def stage3(i):
-        n = block(i)
         for d in range(1, 4):
-            arrive(y.at[n, core, lax.rem(zl + 4 - d, 4)], ags.at[i, d - 1], agr.at[i, d - 1])
-        ref = y.at[n, core]
+            arrive(y.at[i, core, lax.rem(zl + 4 - d, 4)], ags.at[i, d - 1], agr.at[i, d - 1])
+        ref = y.at[i, core]
         send(ref, ref, cgs.at[i], cgr.at[i], other)
 
     def stage4(i):
-        n = block(i)
-        arrive(y.at[n, 1 - core], cgs.at[i], cgr.at[i])
-
-    def y_block(i):
-        return y[block(i)].reshape(TOK, BLK)
-
-    first_rows = (
-        lax.broadcasted_iota(jnp.int32, (SEL, BLK), 0)
-        == lax.broadcasted_iota(jnp.int32, (SEL, BLK), 1)
-    ).astype(F32).astype(BF)
-
-    def pick_y(i):
-        n = block(i)
-        sely[n] = lax.dot_general(first_rows, y_block(i), NT, preferred_element_type=F32).astype(BF)
-
-    def forward(blocks):
-        total = None
-        for i in blocks:
-            n = block(i)
-            term = lax.dot_general(y_block(i), w2g[n], NT, preferred_element_type=F32)
-            total = term if total is None else total + term
-        return total
+        arrive(y.at[i, 1 - core], cgs.at[i], cgr.at[i])
+
+    def rows_at(start):
+        return (
+            lax.broadcasted_iota(jnp.int32, (SEL, BLK), 0) + start
+            == lax.broadcasted_iota(jnp.int32, (SEL, BLK), 1)
+        ).astype(F32).astype(BF)
+
+    first_rows = rows_at(0)
+    other_rows = rows_at(HALF)
+
+    def y_group(g):
+        return y[g].reshape(TOK, BLK)
+
+    def back(step):
+        return lax.rem(r + 8 - step, 8)
+
+    def ahead(step):
+        return lax.rem(r + step, 8)
+
+    def pick_y(n, g, rows):
+        sely[n] = lax.dot_general(rows, y_group(g), NT, preferred_element_type=F32).astype(BF)
+
+    def pick_pair(step):
+        pick_y(back(step), 2 * step - 1, first_rows)
+        pick_y(ahead(step), 2 * step, other_rows)
+
+    def pick_w(n):
+        selw[n] = lax.dot_general(first_rows, w2g[n], NT, preferred_element_type=F32).astype(BF)
+
+    def product(values, n):
+        return lax.dot_general(values, w2g[n], NT, preferred_element_type=F32)
+
+    def pair(step):
+        low, high = y_group(2 * step - 1), y_group(2 * step)
+        behind = jnp.concatenate([low[:, :HALF], high[:, :HALF]], axis=1)
+        before = jnp.concatenate([high[:, HALF:], low[:, HALF:]], axis=1)
+        return product(behind, back(step)) + product(before, ahead(step))
 
     def prepare():
         keep_row = (ids[...] != 0).astype(F32)
@@ -244,109 +269,100 @@
             axis=1, keepdims=True,
         )
         up[...] = (up[...].astype(F32) * keep_col).astype(BF)
-        own_rows = (
-            lax.broadcasted_iota(jnp.int32, (SEL, BLK), 0) + SEL * t
-            == lax.broadcasted_iota(jnp.int32, (SEL, BLK), 1)
-        ).astype(F32).astype(BF)
-        stt[...] = lax.dot_general(own_rows, st[...], NT, preferred_element_type=F32) * keep_row
-        pc1[...] = lax.dot_general(first_rows, w1g[r], NT, preferred_element_type=F32)
+        stt[...] = lax.dot_general(rows_at(SEL * t), st[...], NT, preferred_element_type=F32) * keep_row
+        pc1[...] = lax.dot_general(first_rows[:, :HALF], w1g[r, 0], NT, preferred_element_type=F32)
         pc2[...] = lax.dot_general(first_rows, w2g[c], NT, preferred_element_type=F32)
 
     stage0(0)
     prepare()
     stage1(0)
-    stage2(0)
-    for way in range(2):
-        w1_wait(way, 0, 0)
-        w1_send(way, 1, 0)
+
+    ring(1)
     for way in range(2):
         w2_wait(0, way, 0)
         w2_send(0, way, 2)
+    stage0(1)
+    stage2(0)
+    stage1(1)
+    send_counts()
+
+    ring(2)
+    stage0(2)
+    for way in range(2):
+        z_second(way)
+    stage2(1)
     stage3(0)
-    for way in range(2):
-        w1_wait(way, 0, 1)
-        w1_send(way, 1, 1)
-    stage0(1)
-    stage0(2)
-    for way in range(2):
-        z_second(way)
+    stage1(2)
+    for way in range(2):
+        w2_wait(0, way, 1)
     stage4(0)
-    pick_y(0)
-    stage1(1)
-    stage1(2)
-    for way in range(2):
-        w2_wait(0, way, 1)
-    for way in range(2):
-        w1_wait(way, 1, 0)
-        w1_send(way, 2, 0)
-    stage2(1)
+    pick_y(r, 0, first_rows)
+
+    ring(3)
+    stage0(3)
     stage2(2)
+    stage3(1)
+    stage1(3)
+    stage4(1)
     for way in range(2):
         w2_wait(0, way, 2)
-    stage3(1)
+
+    ring(4)
+    stage0(4)
+    stage2(3)
     stage3(2)
-    for way in range(2):
-        w1_wait(way, 1, 1)
-        w1_send(way, 2, 1)
-    stage0(3)
-    stage0(4)
-    stage4(1)
+    stage1(4)
     stage4(2)
-    pick_y(1)
-    pick_y(2)
-    stage1(3)
-    stage1(4)
     for way in range(2):
         z_wait(way)
     for j in range(2):
         for way in range(2):
             w2_send(1, way, j)
-    for way in range(2):
-        w1_wait(way, 2, 0)
-        w1_send(way, 3, 0)
-    stage2(3)
+    pick_pair(1)
+    for k in range(4):
+        pick_w(2 * k + zh)
+
+    ring(5)
+    stage0(5)
     stage2(4)
     stage3(3)
-    stage3(4)
+    stage1(5)
+    stage4(3)
     for way in range(2):
         w2_wait(1, way, 0)
         w2_send(1, way, 2)
-    for way in range(2):
-        w1_wait(way, 2, 1)
-    stage0(5)
+
+    ring(6)
     stage0(6)
-    stage4(3)
+    stage2(5)
+    stage3(4)
+    stage1(6)
     stage4(4)
-    pick_y(3)
-    pick_y(4)
-    stage1(5)
-    stage1(6)
-    for way in range(2):
-        w1_wait(way, 3, 0)
+    pick_pair(2)
+
+    ring(7)
     stage0(7)
-    stage2(5)
     stage2(6)
     stage1(7)
     stage3(5)
+    stage4(5)
+    for way in range(2):
+        w2_wait(1, way, 1)
+        w2_wait(1, way, 2)
+    for k in range(4):
+        pick_w(2 * k + 1 - zh)
     stage3(6)
+    pre2[...] = product(y_group(0), r) + pair(1)
     stage2(7)
-    stage4(5)
     stage4(6)
-    pick_y(5)
-    pick_y(6)
-    for way in range(2):
-        w2_wait(1, way, 1)
-    for way in range(2):
-        w2_wait(1, way, 2)
-    for n in range(8):
-        selw[n] = lax.dot_general(first_rows, w2g[n], NT, preferred_element_type=F32).astype(BF)
+    pre2[...] += pair(2)
+    pick_pair(3)
+    pre2[...] += pair(3)
     stage3(7)
-    pre2[...] = forward(range(7))
     stage4(7)
-    pick_y(7)
-
-    last = block(7)
-    y_last = y_block(7)
+
+    last = ahead(4)
+    y_last = y_group(7)
     carried = jnp.zeros((BLK, TOK), F32)
     for k in range(4):
         cols = slice(256 * k, 256 * k + 256)
@@ -364,6 +380,7 @@
     for d in range(1, 8):
         send(q.at[lax.rem(t + d, 8)], qin.at[d - 1], qs.at[d - 1], qr.at[d - 1], tp_dev(d))
 
+    pick_y(last, 7, first_rows)
     factor = weight * INNER
     grad = jnp.dot(sely[...].reshape(BLK, TOK), slope[...], preferred_element_type=F32) * SCALE_MODEL
     t2[...] = (factor * grad).astype(BF).reshape(4, 2, SEL, HID)
@@ -382,8 +399,15 @@
         arrive(dy.at[lax.rem(t + 8 - d, 8)], ds_.at[d - 1], dr_.at[d - 1])
     grad = jnp.dot(dy[...].reshape(BLK, TOK), act[...], preferred_element_type=F32) * SCALE_HIDDEN
     t1[...] = (factor * grad).astype(BF).reshape(8, SEL, HID)
-    for d in (4, 3, 5, 2, 6, 1, 7):
+
+    def row_send(d):
         send(t1.at[lax.rem(r + d, 8)], t1in.at[d - 1], rs_.at[d - 1], rr_.at[d - 1], row_dev(d))
+
+    joint = jnp.where(core == 0, 5, 3)
+    send(t1.at[lax.rem(r + 4, 8)], t1in.at[3], rs_.at[3], rr_.at[3], row_dev(jnp.where(core == 0, 7, 1)))
+    row_send(8 - joint)
+    for d in (2, 6, 1, 7):
+        row_send(d)
 
     far = t2[x, 1 - zh].astype(F32)
     near = t2[x, zh].astype(F32)
@@ -394,6 +418,11 @@
     t2z[...] = far.astype(BF)
     send(t2z, t2zin, as_, ar_, antipode)
 
+    arrive(t1in.at[3], rs_.at[3], rr_.at[3])
+    to = lax.rem(r + joint, 8)
+    t1[to] = (t1[to].astype(F32) + t1in[3].astype(F32)).astype(BF)
+    row_send(joint)
+
     def total_of(buffer, s_sems, r_sems):
         count = wown[...]
         for d in range(1, 8):
@@ -411,7 +440,7 @@
     o2[...] = pc2[...] - OUTER * (delta + DECAY * moment)
 
     summed = t1[r].astype(F32)
-    for d in (1, 7, 2, 6, 3, 5, 4):
+    for d in (1, 7, 2, 6, 3, 5):
         arrive(t1in.at[d - 1], rs_.at[d - 1], rr_.at[d - 1])
         summed = summed + t1in[d - 1].astype(F32)
     delta = summed / total_one
@@ -423,17 +452,21 @@
         copy.wait_send()
 
 
+def in_hbm(value):
+    return pltpu.with_memory_space_constraint(value, pltpu.HBM)
+
+
 def on_device(
     act_one, residual, upstream, stream_grad, token_ids, shard_counts,
     out_one, in_two, out_one_moment, in_two_moment,
 ):
     dma = pltpu.SemaphoreType.DMA
     vmem = pltpu.VMEM
-    whole = pl.BlockSpec(memory_space=pl.ANY)
+    whole = pl.BlockSpec(memory_space=pltpu.HBM)
     inside = pl.BlockSpec(memory_space=pltpu.VMEM)
     scratch = [
         vmem((TOK, HID), BF), vmem((TOK, BLK), BF), vmem((TOK, HID), BF), vmem((TOK, BLK), BF),
-        vmem((1, TOK), jnp.int32), vmem((8, HID, BLK), BF), vmem((8, HID, BLK), BF),
+        vmem((1, TOK), jnp.int32), vmem((8, 2, HID, HALF), BF), vmem((8, HID, BLK), BF),
         vmem((SEL, HID), F32), vmem((SEL, HID), F32),
         vmem((8, 2, 128, BLK), BF), vmem((8, 128, BLK), BF),
         vmem((8, 4, SEL, BLK), BF), vmem((8, 3, SEL, BLK), BF),
@@ -445,7 +478,7 @@
         vmem((4, 2, SEL, HID), BF), vmem((3, 2, SEL, HID), BF),
         vmem((SEL, HID), BF), vmem((SEL, HID), BF),
         vmem((8, 128), F32), vmem((7, 8, 128), F32), vmem((7, 8, 128), F32),
-        dma((9,)),
+        dma((10,)),
         dma((2, 4, 2)), dma((2, 4, 2)), dma((2, 2, 3)), dma((2, 2, 3)), dma((2, 2)), dma((2, 2)),
         dma((8,)), dma((8,)), dma((8, 3)), dma((8, 3)), dma((8, 3)), dma((8, 3)), dma((8,)), dma((8,)),
         dma((7,)), dma((7,)), dma((7,)), dma((7,)), dma((7,)), dma((7,)),
@@ -463,8 +496,9 @@
         ),
         cost_estimate=pl.CostEstimate(flops=3_000_000_000, bytes_accessed=4_000_000, transcendentals=300_000),
     )(
-        act_one[0, 0], residual[0, 0], upstream[0, 0], stream_grad[0, 0], token_ids[0],
-        shard_counts, out_one[0], in_two[0], out_one_moment[0].T, in_two_moment[0].T,
+        *map(in_hbm, (act_one[0, 0], residual[0, 0], upstream[0, 0], stream_grad[0, 0], token_ids[0])),
+        shard_counts,
+        *map(in_hbm, (out_one[0], in_two[0], out_one_moment[0].T, in_two_moment[0].T)),
     )
     return (o1.T[None], n1.T[None], o2.T[None], n2.T[None])
 

time: 121 us -> 108 us (0.89)
  local copies, waits for them, and re-layouts: 11.1 us -> 2.62 us
  Pallas kernels: 109 us -> 103 us
    unnamed x22 -> x4, local copies, waits for them, and re-layouts: 11.1 us -> 2.62 us
    pallas_call x1, Pallas kernels: 109 us -> 103 us  [on_device(): pl.pallas_call(kernel, out_shape=(result,) * 4, in_specs=[whole] * 5 + [i...]
where the time goes in v2:
time: 108 us; the launch traced here: 107 us
  Pallas kernels  103 us (95%)
  local copies, waits for them, and re-layouts  2.62 us (2%)
  between operations  1.29 us (1%)
    pallas_call x1, Pallas kernels, on_device(): pl.pallas_call(kernel, out_shape=(result,) * 4, in_specs=[whole] * 5 + [i...  103 us
    unnamed x4, local copies, waits for them, and re-layouts  2.62 us

profile of v2, /device:TPU:1, one launch (start us, length us, event | category | flops | bytes accessed | tf_op | source)
XLA Modules:
  0.0 107.2 jit_solution(2928277115983600083)
XLA Ops:
  1.3 103.3 %shard_map.129 = (f32[32,1024]{1,0:T(8,128)S(1)}, f32[32,1024]{1,0:T(8,128)S(1)}, f32[32,1024]{1,0:T(8,128)S(1)}, f32[32,1024]{1,0:T(8,128)S(1)}) custom-call(bf16[256,1024]{1,0:T(8,128)(2,1)} %bitcast.29, bf16[256,256]{1,0:T(8,128)(2,1)} %bitcast.33, bf16[256,1024]{1,0:T(8,128)(2,1)} %bitcast.30, bf16[256,256]{1,0:T(8,128)(2,1)} %bitcast.34, ...), custom_call_target="tpu_custom_call" | custom-call | flops 3000000000 | bytes 4000000 | tf_op jit(solution)/shard_map/pallas_call | solution.py:488
  104.6 0.7 copy.19
  105.2 0.7 copy.20
  105.9 0.7 copy.21
  106.5 0.7 copy.22

commit v3 on v2

--- a/solution.py
+++ b/solution.py
@@ -30,10 +30,10 @@
     act_h, res_h, up_h, st_h, ids_h, cnt_v, w1_h, w2_h, m1_h, m2_h,
     o1, n1, o2, n2,
     act, res, up, st, ids, w1g, w2g, m1, m2,
-    part, cin, zb, zin, y, relay, pre2, slope, selw, sely, stt, pc1, pc2,
+    part, cin, lin, zb, zin, y, relay, pre2, slope, selw, sely, stt, pc1, pc2,
     q, qin, dy, t1, t1in, t2, t2x, t2z, t2zin, wown, wrow, wcol,
     loc, w1s, w1r, w2s, w2r, zs, zr,
-    crs, crr, zrs, zrr, ags, agr, cgs, cgr,
+    crs, crr, zrs, zrr, ags, agr, cgs, cgr, lrs, lrr, lgs, lgr,
     qs, qr, ds_, dr_, rs_, rr_, xs, xr, as_, ar_, nrs, nrr, ncs, ncr,
 ):
     r = lax.axis_index("row")
@@ -96,16 +96,10 @@
         copy.start()
 
     barrier = pltpu.get_barrier_semaphore()
-    partners = (
-        [row_dev(d) for d in range(1, 8)]
-        + [col_dev(d) for d in range(1, 8)]
-        + [tp_dev(d) for d in range(1, 8)]
-        + [z_dev(2), z_dev(6)]
-    )
+    partners = [row_dev(1), row_dev(7), x_dev(1), x_dev(3), z_dev(2), z_dev(6), other]
+    partners += [zl_dev(d) for d in range(1, 4)]
     for device in partners:
         pl.semaphore_signal(barrier, inc=1, device_id=device, device_id_type=MESH)
-    weight = cnt_v[...].astype(F32)
-    wown[...] = jnp.broadcast_to(weight, (8, 128))
     pl.semaphore_wait(barrier, len(partners))
 
     def chunk(way, step, j):
@@ -122,40 +116,53 @@
             if step < 2 or (step == 2 and j == 0):
                 w1_send(way, step + 1, j)
 
-    def w2_chunk(at, phase, half):
-        plane = zh if phase == 0 else 1 - zh
-        return w2g.at[lax.rem(at, 4) * 2 + plane, pl.ds(512 * half, 512)]
-
-    def w2_send(phase, way, j):
-        half = j % 2 if way == 0 else 1 - j % 2
-        back = 0 if j < 2 else 1
-        at = x + (4 - back if way == 0 else back)
-        ref = w2_chunk(at, phase, half)
-        send(ref, ref, w2s.at[phase, way, j], w2r.at[phase, way, j], x_dev(1 if way == 0 else 3))
-
-    def w2_wait(phase, way, j):
-        half = j % 2 if way == 0 else 1 - j % 2
-        back = 1 if j < 2 else 2
-        at = x + (4 - back if way == 0 else back)
-        arrive(w2_chunk(at, phase, half), w2s.at[phase, way, j], w2r.at[phase, way, j])
-
-    def z_first(way):
+    def near_half(at, half):
+        return w2g.at[lax.rem(at, 4) * 2 + zh, pl.ds(512 * half, 512)]
+
+    def far_quarter(at, quarter):
+        return w2g.at[lax.rem(at, 4) * 2 + 1 - zh, pl.ds(256 * quarter, 256)]
+
+    def near_part(way, e, hops):
+        half = (0, 1, 0)[e] if way == 0 else (1, 0, 1)[e]
+        steps = hops + (1 if e == 2 else 0)
+        return near_half(x + (4 - steps if way == 0 else steps), half)
+
+    def far_part(way, e, hops):
+        quarter = (0, 2, 1, 3, 0, 1)[e] if way == 0 else (2, 0, 3, 1, 2, 3)[e]
+        steps = hops + (1 if e > 3 else 0)
+        return far_quarter(x + (4 - steps if way == 0 else steps), quarter)
+
+    def near_send(way, e):
+        ref = near_part(way, e, 0)
+        send(ref, ref, w2s.at[way, e], w2r.at[way, e], x_dev(1 if way == 0 else 3))
+
+    def near_wait(way, e):
+        arrive(near_part(way, e, 1), w2s.at[way, e], w2r.at[way, e])
+
+    def far_send(way, e):
+        ref = far_part(way, e, 0)
+        send(ref, ref, w2s.at[way, 3 + e], w2r.at[way, 3 + e], x_dev(1 if way == 0 else 3))
+
+    def far_wait(way, e):
+        arrive(far_part(way, e, 1), w2s.at[way, 3 + e], w2r.at[way, 3 + e])
+
+    def z_first(way, e):
         send(
-            w2g.at[c, pl.ds(512 * way, 512)], relay.at[way],
-            zs.at[way, 0], zr.at[way, 0], z_dev(2 if way == 0 else 6),
-        )
-
-    def z_second(way):
-        arrive(relay.at[way], zs.at[way, 0], zr.at[way, 0])
+            w2g.at[c, pl.ds(512 * way + 256 * e, 256)], relay.at[way, e],
+            zs.at[way, e, 0], zr.at[way, e, 0], z_dev(2 if way == 0 else 6),
+        )
+
+    def z_second(way, e):
+        arrive(relay.at[way, e], zs.at[way, e, 0], zr.at[way, e, 0])
         hop = 2 if way == 0 else 6
         far = lax.div(lax.rem(z + hop, 8), 4)
         send(
-            relay.at[way], w2g.at[x * 2 + 1 - far, pl.ds(512 * way, 512)],
-            zs.at[way, 1], zr.at[way, 1], z_dev(hop),
-        )
-
-    def z_wait(way):
-        arrive(w2g.at[x * 2 + 1 - zh, pl.ds(512 * way, 512)], zs.at[way, 1], zr.at[way, 1])
+            relay.at[way, e], w2g.at[x * 2 + 1 - far, pl.ds(512 * way + 256 * e, 256)],
+            zs.at[way, e, 1], zr.at[way, e, 1], z_dev(hop),
+        )
+
+    def z_wait(way, e):
+        arrive(far_quarter(x, 2 * way + e), zs.at[way, e, 1], zr.at[way, e, 1])
 
     local[0].wait()
     local[1].wait()
@@ -163,13 +170,15 @@
         for way in range(2):
             w1_send(way, 0, j)
     local[2].wait()
-    for j in range(2):
+    for e in range(2):
         for way in range(2):
-            w2_send(0, way, j)
-    for way in range(2):
-        z_first(way)
+            z_first(way, e)
+            near_send(way, e)
     for copy in local[3:]:
         copy.wait()
+
+    weight = cnt_v[...].astype(F32)
+    wown[...] = jnp.broadcast_to(weight, (8, 128))
 
     def send_counts():
         for d in range(1, 8):
@@ -182,7 +191,7 @@
         second = chunk(1, step, j)
         return first, second
 
-    def stage0(g):
+    def partial_sum(g):
         (na, ha), (nb, hb) = group(g)
         rhs = jnp.concatenate([w1g[na, ha], w1g[nb, hb]], axis=1)
         acc = jnp.dot(act[...], rhs, preferred_element_type=F32) * SCALE_HIDDEN
@@ -191,13 +200,16 @@
             mine = jnp.where(n == t, 1.0, 0.0).astype(F32)
             own.append(res[:, HALF * half : HALF * half + HALF].astype(F32) * mine)
         acc = acc + jnp.concatenate(own, axis=1)
-        part[g] = acc.astype(BF).reshape(2, 128, BLK)
+        part[g] = acc.astype(BF).reshape(2, 4, SEL, BLK)
+
+    def stage0(g):
+        partial_sum(g)
         send(part.at[g, 1 - core], cin.at[g], crs.at[g], crr.at[g], other)
 
     def stage1(i):
         arrive(cin.at[i], crs.at[i], crr.at[i])
         both = part[i, core].astype(F32) + cin[i].astype(F32)
-        zb[i] = both.astype(BF).reshape(4, SEL, BLK)
+        zb[i] = both.astype(BF)
         for d in range(1, 4):
             send(
                 zb.at[i, lax.rem(zl + d, 4)], zin.at[i, d - 1],
@@ -223,6 +235,29 @@
     def stage4(i):
         arrive(y.at[i, 1 - core], cgs.at[i], cgr.at[i])
 
+    def place(d):
+        at = lax.rem(t + d, 8)
+        return lax.rem(at, 2), lax.div(at, 2)
+
+    def last_out():
+        partial_sum(7)
+        for d in range(1, 8):
+            send(part.at[(7, *place(d))], lin.at[d - 1], lrs.at[d - 1], lrr.at[d - 1], tp_dev(d))
+
+    def last_back():
+        total = part[7, core, zl].astype(F32)
+        for d in range(1, 8):
+            arrive(lin.at[d - 1], lrs.at[d - 1], lrr.at[d - 1])
+            total = total + lin[d - 1].astype(F32)
+        y[7, core, zl] = total.astype(BF)
+        for d in range(1, 8):
+            ref = y.at[7, core, zl]
+            send(ref, ref, lgs.at[d - 1], lgr.at[d - 1], tp_dev(d))
+
+    def last_wait():
+        for d in range(1, 8):
+            arrive(y.at[(7, *place(8 - d))], lgs.at[d - 1], lgr.at[d - 1])
+
     def rows_at(start):
         return (
             lax.broadcasted_iota(jnp.int32, (SEL, BLK), 0) + start
@@ -279,87 +314,95 @@
 
     ring(1)
     for way in range(2):
-        w2_wait(0, way, 0)
-        w2_send(0, way, 2)
+        z_second(way, 0)
+    for way in range(2):
+        near_wait(way, 0)
+        near_send(way, 2)
     stage0(1)
+    stage1(1)
+
+    ring(2)
+    for way in range(2):
+        z_second(way, 1)
+    stage0(2)
     stage2(0)
-    stage1(1)
-    send_counts()
-
-    ring(2)
-    stage0(2)
-    for way in range(2):
-        z_second(way)
+    stage1(2)
+    for way in range(2):
+        near_wait(way, 1)
+
+    ring(3)
+    stage0(3)
     stage2(1)
+    stage1(3)
+    for way in range(2):
+        near_wait(way, 2)
+    for k in range(4):
+        pick_w(2 * k + zh)
+    for way in range(2):
+        z_wait(way, 0)
+    for e in range(2):
+        for way in range(2):
+            far_send(way, e)
+
+    ring(4)
+    stage0(4)
+    stage2(2)
     stage3(0)
-    stage1(2)
-    for way in range(2):
-        w2_wait(0, way, 1)
+    stage1(4)
     stage4(0)
     pick_y(r, 0, first_rows)
-
-    ring(3)
-    stage0(3)
-    stage2(2)
+    for way in range(2):
+        z_wait(way, 1)
+    for e in range(2, 4):
+        for way in range(2):
+            far_send(way, e)
+
+    ring(5)
+    for way in range(2):
+        far_wait(way, 0)
+        far_send(way, 4)
+    stage0(5)
+    stage2(3)
     stage3(1)
-    stage1(3)
+    stage1(5)
     stage4(1)
-    for way in range(2):
-        w2_wait(0, way, 2)
-
-    ring(4)
-    stage0(4)
-    stage2(3)
+
+    ring(6)
+    for way in range(2):
+        far_wait(way, 2)
+        far_send(way, 5)
+    stage0(6)
+    stage2(4)
     stage3(2)
-    stage1(4)
+    stage1(6)
+    stage2(5)
     stage4(2)
-    for way in range(2):
-        z_wait(way)
-    for j in range(2):
-        for way in range(2):
-            w2_send(1, way, j)
     pick_pair(1)
-    for k in range(4):
-        pick_w(2 * k + zh)
-
-    ring(5)
-    stage0(5)
-    stage2(4)
+
+    ring(7)
+    last_out()
+    stage2(6)
     stage3(3)
-    stage1(5)
+    stage3(4)
     stage4(3)
-    for way in range(2):
-        w2_wait(1, way, 0)
-        w2_send(1, way, 2)
-
-    ring(6)
-    stage0(6)
-    stage2(5)
-    stage3(4)
-    stage1(6)
     stage4(4)
     pick_pair(2)
-
-    ring(7)
-    stage0(7)
-    stage2(6)
-    stage1(7)
     stage3(5)
-    stage4(5)
-    for way in range(2):
-        w2_wait(1, way, 1)
-        w2_wait(1, way, 2)
+    for way in range(2):
+        for e in (1, 3, 4, 5):
+            far_wait(way, e)
+    send_counts()
+    stage3(6)
+    last_back()
     for k in range(4):
         pick_w(2 * k + 1 - zh)
-    stage3(6)
     pre2[...] = product(y_group(0), r) + pair(1)
-    stage2(7)
+    pre2[...] += pair(2)
+    stage4(5)
     stage4(6)
-    pre2[...] += pair(2)
+    pre2[...] += pair(3)
     pick_pair(3)
-    pre2[...] += pair(3)
-    stage3(7)
-    stage4(7)
+    last_wait()
 
     last = ahead(4)
     y_last = y_group(7)
@@ -452,6 +495,17 @@
         copy.wait_send()
 
 
+def write_out(a, b, c, d, a_out, b_out, c_out, d_out, sems):
+    copies = [
+        pltpu.make_async_copy(src, dst, sems.at[k])
+        for k, (src, dst) in enumerate(((a, a_out), (b, b_out), (c, c_out), (d, d_out)))
+    ]
+    for copy in copies:
+        copy.start()
+    for copy in copies:
+        copy.wait()
+
+
 def in_hbm(value):
     return pltpu.with_memory_space_constraint(value, pltpu.HBM)
 
@@ -468,9 +522,9 @@
         vmem((TOK, HID), BF), vmem((TOK, BLK), BF), vmem((TOK, HID), BF), vmem((TOK, BLK), BF),
         vmem((1, TOK), jnp.int32), vmem((8, 2, HID, HALF), BF), vmem((8, HID, BLK), BF),
         vmem((SEL, HID), F32), vmem((SEL, HID), F32),
-        vmem((8, 2, 128, BLK), BF), vmem((8, 128, BLK), BF),
-        vmem((8, 4, SEL, BLK), BF), vmem((8, 3, SEL, BLK), BF),
-        vmem((8, 2, 4, SEL, BLK), BF), vmem((2, 512, BLK), BF),
+        vmem((8, 2, 4, SEL, BLK), BF), vmem((7, 4, SEL, BLK), BF), vmem((7, SEL, BLK), BF),
+        vmem((7, 4, SEL, BLK), BF), vmem((7, 3, SEL, BLK), BF),
+        vmem((8, 2, 4, SEL, BLK), BF), vmem((2, 2, BLK, BLK), BF),
         vmem((TOK, HID), F32), vmem((TOK, HID), BF), vmem((8, SEL, HID), BF),
         vmem((8, SEL, TOK), BF), vmem((SEL, TOK), F32), vmem((SEL, HID), F32), vmem((SEL, HID), F32),
         vmem((8, SEL, TOK), BF), vmem((7, SEL, TOK), BF), vmem((8, SEL, TOK), BF),
@@ -479,8 +533,9 @@
         vmem((SEL, HID), BF), vmem((SEL, HID), BF),
         vmem((8, 128), F32), vmem((7, 8, 128), F32), vmem((7, 8, 128), F32),
         dma((10,)),
-        dma((2, 4, 2)), dma((2, 4, 2)), dma((2, 2, 3)), dma((2, 2, 3)), dma((2, 2)), dma((2, 2)),
-        dma((8,)), dma((8,)), dma((8, 3)), dma((8, 3)), dma((8, 3)), dma((8, 3)), dma((8,)), dma((8,)),
+        dma((2, 4, 2)), dma((2, 4, 2)), dma((2, 9)), dma((2, 9)), dma((2, 2, 2)), dma((2, 2, 2)),
+        dma((7,)), dma((7,)), dma((7, 3)), dma((7, 3)), dma((7, 3)), dma((7, 3)), dma((7,)), dma((7,)),
+        dma((7,)), dma((7,)), dma((7,)), dma((7,)),
         dma((7,)), dma((7,)), dma((7,)), dma((7,)), dma((7,)), dma((7,)),
         dma((3,)), dma((3,)), dma(()), dma(()), dma((7,)), dma((7,)), dma((7,)), dma((7,)),
     ]
@@ -500,6 +555,14 @@
         shard_counts,
         *map(in_hbm, (out_one[0], in_two[0], out_one_moment[0].T, in_two_moment[0].T)),
     )
+    o1, n1, o2, n2 = pl.pallas_call(
+        write_out,
+        out_shape=(result,) * 4,
+        in_specs=[pl.BlockSpec(memory_space=pl.ANY)] * 4,
+        out_specs=(whole,) * 4,
+        scratch_shapes=[dma((4,))],
+        compiler_params=pltpu.CompilerParams(vmem_limit_bytes=1024 * 1024),
+    )(o1, n1, o2, n2)
     return (o1.T[None], n1.T[None], o2.T[None], n2.T[None])
 
 

time: 108 us -> 95.2 us (0.88)
  Pallas kernels: 103 us -> 93.7 us
  local copies, waits for them, and re-layouts: 2.62 us -> 0 us
    pallas_call x1, Pallas kernels: 103 us -> 92.9 us  [on_device(): pl.pallas_call(kernel, out_shape=(result,) * 4, in_specs=[whole] * 5 + [i...]
    unnamed x4 -> x0, local copies, waits for them, and re-layouts: 2.62 us -> none
where the time goes in v3:
time: 95.2 us; the launch traced here: 95 us
  Pallas kernels  93.7 us (98%)
  between operations  1.29 us (1%)
    pallas_call x1, Pallas kernels, on_device(): pl.pallas_call(kernel, out_shape=(result,) * 4, in_specs=[whole] * 5 + [i...  92.9 us

profile of v3, /device:TPU:1, one launch (start us, length us, event | category | flops | bytes accessed | tf_op | source)
XLA Modules:
  0.0 95.0 jit_solution(10098309166009428813)
XLA Ops:
  1.3 92.9 %shard_map.129 = (f32[32,1024]{1,0:T(8,128)S(1)}, f32[32,1024]{1,0:T(8,128)S(1)}, f32[32,1024]{1,0:T(8,128)S(1)}, f32[32,1024]{1,0:T(8,128)S(1)}) custom-call(bf16[256,1024]{1,0:T(8,128)(2,1)} %bitcast.25, bf16[256,256]{1,0:T(8,128)(2,1)} %bitcast.29, bf16[256,1024]{1,0:T(8,128)(2,1)} %bitcast.26, bf16[256,256]{1,0:T(8,128)(2,1)} %bitcast.30, ...), custom_call_target="tpu_custom_call" | custom-call | flops 3000000000 | bytes 4000000 | tf_op jit(solution)/shard_map/pallas_call | solution.py:543
  94.2 0.8 shard_map.130

commit v4 on v3

--- a/solution.py
+++ b/solution.py
@@ -82,6 +82,11 @@
             device_id=other, device_id_type=MESH,
         ).wait_recv()
 
+    barrier = pltpu.get_barrier_semaphore()
+    partners = [row_dev(1), row_dev(7), x_dev(1), x_dev(3), z_dev(2), z_dev(6), other]
+    partners += [zl_dev(d) for d in range(1, 4)]
+    for device in partners:
+        pl.semaphore_signal(barrier, inc=1, device_id=device, device_id_type=MESH)
     local = [
         pltpu.make_async_copy(a, b, loc.at[k])
         for k, (a, b) in enumerate(
@@ -95,11 +100,6 @@
     for copy in local:
         copy.start()
 
-    barrier = pltpu.get_barrier_semaphore()
-    partners = [row_dev(1), row_dev(7), x_dev(1), x_dev(3), z_dev(2), z_dev(6), other]
-    partners += [zl_dev(d) for d in range(1, 4)]
-    for device in partners:
-        pl.semaphore_signal(barrier, inc=1, device_id=device, device_id_type=MESH)
     pl.semaphore_wait(barrier, len(partners))
 
     def chunk(way, step, j):
@@ -310,7 +310,6 @@
 
     stage0(0)
     prepare()
-    stage1(0)
 
     ring(1)
     for way in range(2):
@@ -319,81 +318,80 @@
         near_wait(way, 0)
         near_send(way, 2)
     stage0(1)
-    stage1(1)
 
     ring(2)
+    stage0(2)
     for way in range(2):
         z_second(way, 1)
-    stage0(2)
-    stage2(0)
-    stage1(2)
+    stage1(0)
     for way in range(2):
         near_wait(way, 1)
 
     ring(3)
     stage0(3)
-    stage2(1)
-    stage1(3)
+    stage1(1)
+    stage1(2)
     for way in range(2):
         near_wait(way, 2)
     for k in range(4):
         pick_w(2 * k + zh)
+
+    ring(4)
+    stage0(4)
+    stage2(0)
+    stage1(3)
     for way in range(2):
         z_wait(way, 0)
     for e in range(2):
         for way in range(2):
             far_send(way, e)
-
-    ring(4)
-    stage0(4)
+    stage2(1)
+    stage1(4)
+
+    ring(5)
+    stage0(5)
     stage2(2)
-    stage3(0)
-    stage1(4)
-    stage4(0)
-    pick_y(r, 0, first_rows)
     for way in range(2):
         z_wait(way, 1)
     for e in range(2, 4):
         for way in range(2):
             far_send(way, e)
-
-    ring(5)
+    stage3(0)
+    stage2(3)
+    stage1(5)
+    stage3(1)
+    stage4(0)
+    pick_y(r, 0, first_rows)
+
+    ring(6)
     for way in range(2):
         far_wait(way, 0)
         far_send(way, 4)
-    stage0(5)
-    stage2(3)
-    stage3(1)
-    stage1(5)
-    stage4(1)
-
-    ring(6)
-    for way in range(2):
-        far_wait(way, 2)
-        far_send(way, 5)
     stage0(6)
+    stage1(6)
     stage2(4)
     stage3(2)
-    stage1(6)
+    stage4(1)
     stage2(5)
     stage4(2)
     pick_pair(1)
 
     ring(7)
     last_out()
+    for way in range(2):
+        far_wait(way, 2)
+        far_send(way, 5)
     stage2(6)
     stage3(3)
     stage3(4)
     stage4(3)
     stage4(4)
-    pick_pair(2)
     stage3(5)
+    last_back()
+    stage3(6)
     for way in range(2):
         for e in (1, 3, 4, 5):
             far_wait(way, e)
-    send_counts()
-    stage3(6)
-    last_back()
     for k in range(4):
         pick_w(2 * k + 1 - zh)
     pre2[...] = product(y_group(0), r) + pair(1)
@@ -401,7 +399,6 @@
     stage4(5)
     stage4(6)
     pre2[...] += pair(3)
-    pick_pair(3)
     last_wait()
 
     last = ahead(4)
@@ -423,6 +420,8 @@
     for d in range(1, 8):
         send(q.at[lax.rem(t + d, 8)], qin.at[d - 1], qs.at[d - 1], qr.at[d - 1], tp_dev(d))
 
+    pick_pair(2)
+    pick_pair(3)
     pick_y(last, 7, first_rows)
     factor = weight * INNER
     grad = jnp.dot(sely[...].reshape(BLK, TOK), slope[...], preferred_element_type=F32) * SCALE_MODEL
@@ -438,6 +437,7 @@
     for d in range(1, 8):
         ref = dy.at[t]
         send(ref, ref, ds_.at[d - 1], dr_.at[d - 1], tp_dev(d))
+    send_counts()
     for d in range(1, 8):
         arrive(dy.at[lax.rem(t + 8 - d, 8)], ds_.at[d - 1], dr_.at[d - 1])
     grad = jnp.dot(dy[...].reshape(BLK, TOK), act[...], preferred_element_type=F32) * SCALE_HIDDEN
@@ -446,11 +446,12 @@
     def row_send(d):
         send(t1.at[lax.rem(r + d, 8)], t1in.at[d - 1], rs_.at[d - 1], rr_.at[d - 1], row_dev(d))
 
+    before_rows = len(pending)
     joint = jnp.where(core == 0, 5, 3)
     send(t1.at[lax.rem(r + 4, 8)], t1in.at[3], rs_.at[3], rr_.at[3], row_dev(jnp.where(core == 0, 7, 1)))
     row_send(8 - joint)
-    for d in (2, 6, 1, 7):
-        row_send(d)
+    row_send(2)
+    row_send(6)
 
     far = t2[x, 1 - zh].astype(F32)
     near = t2[x, zh].astype(F32)
@@ -465,6 +466,8 @@
     to = lax.rem(r + joint, 8)
     t1[to] = (t1[to].astype(F32) + t1in[3].astype(F32)).astype(BF)
     row_send(joint)
+    row_send(1)
+    row_send(7)
 
     def total_of(buffer, s_sems, r_sems):
         count = wown[...]
@@ -482,8 +485,10 @@
     n2[...] = moment
     o2[...] = pc2[...] - OUTER * (delta + DECAY * moment)
 
+    for copy in pending[:before_rows]:
+        copy.wait_send()
     summed = t1[r].astype(F32)
-    for d in (1, 7, 2, 6, 3, 5):
+    for d in (2, 6, 3, 5, 1, 7):
         arrive(t1in.at[d - 1], rs_.at[d - 1], rr_.at[d - 1])
         summed = summed + t1in[d - 1].astype(F32)
     delta = summed / total_one
@@ -491,7 +496,7 @@
     n1[...] = moment
     o1[...] = pc1[...] - OUTER * (delta + DECAY * moment)
 
-    for copy in pending:
+    for copy in pending[before_rows:]:
         copy.wait_send()
 
 

time: 95.2 us -> 92 us (0.966)
  Pallas kernels: 93.7 us -> 90.5 us
    pallas_call x1, Pallas kernels: 92.9 us -> 89.7 us  [on_device(): pl.pallas_call(kernel, out_shape=(result,) * 4, in_specs=[whole] * 5 + [i...]
where the time goes in v4:
time: 92 us; the launch traced here: 91.8 us
  Pallas kernels  90.5 us (98%)
  between operations  1.29 us (1%)
    pallas_call x1, Pallas kernels, on_device(): pl.pallas_call(kernel, out_shape=(result,) * 4, in_specs=[whole] * 5 + [i...  89.7 us

profile of v4, /device:TPU:1, one launch (start us, length us, event | category | flops | bytes accessed | tf_op | source)
XLA Modules:
  0.0 91.8 jit_solution(7364467752126953753)
XLA Ops:
  1.3 89.7 %shard_map.129 = (f32[32,1024]{1,0:T(8,128)S(1)}, f32[32,1024]{1,0:T(8,128)S(1)}, f32[32,1024]{1,0:T(8,128)S(1)}, f32[32,1024]{1,0:T(8,128)S(1)}) custom-call(bf16[256,1024]{1,0:T(8,128)(2,1)} %bitcast.25, bf16[256,256]{1,0:T(8,128)(2,1)} %bitcast.29, bf16[256,1024]{1,0:T(8,128)(2,1)} %bitcast.26, bf16[256,256]{1,0:T(8,128)(2,1)} %bitcast.30, ...), custom_call_target="tpu_custom_call" | custom-call | flops 3000000000 | bytes 4000000 | tf_op jit(solution)/shard_map/pallas_call | solution.py:548
  91.0 0.8 shard_map.130

commit v5 on v4

--- a/solution.py
+++ b/solution.py
@@ -49,9 +49,6 @@
     def row_dev(d):
         return (lax.rem(r + d, 8), c, t)
 
-    def tp_dev(d):
-        return (r, c, lax.rem(t + d, 8))
-
     def x_dev(d):
         return (r, lax.rem(x + d, 4) * 2 + zh, t)
 
@@ -64,6 +61,16 @@
 
     def col_dev(d):
         return (r, lax.rem(c + d, 8), t)
+
+    end = jnp.where((zl == 0) | (zl == 3), 1, 0)
+    down = jnp.where(zl < 2, 0, 1)
+
+    def peer(p):
+        if p == 6:
+            return zl * 2 + 1 - core
+        far = (3, 2 * end, 2 - end)[p // 2]
+        to = far + down * (3 - 2 * far)
+        return to * 2 + (core if p % 2 == 0 else 1 - core)
 
     antipode = (r, x * 2 + 1 - zh, t)
     pending = []
@@ -235,28 +242,31 @@
     def stage4(i):
         arrive(y.at[i, 1 - core], cgs.at[i], cgr.at[i])
 
-    def place(d):
-        at = lax.rem(t + d, 8)
+    def place(at):
         return lax.rem(at, 2), lax.div(at, 2)
 
     def last_out():
         partial_sum(7)
-        for d in range(1, 8):
-            send(part.at[(7, *place(d))], lin.at[d - 1], lrs.at[d - 1], lrr.at[d - 1], tp_dev(d))
+        for p in range(7):
+            to = peer(p)
+            send(part.at[(7, *place(to))], lin.at[t], lrs.at[to], lrr.at[t], (r, c, to))
 
     def last_back():
         total = part[7, core, zl].astype(F32)
-        for d in range(1, 8):
-            arrive(lin.at[d - 1], lrs.at[d - 1], lrr.at[d - 1])
-            total = total + lin[d - 1].astype(F32)
+        for p in range(6, -1, -1):
+            by = peer(p)
+            arrive(lin.at[by], lrs.at[by], lrr.at[by])
+            total = total + lin[by].astype(F32)
         y[7, core, zl] = total.astype(BF)
-        for d in range(1, 8):
+        for p in range(7):
+            to = peer(p)
             ref = y.at[7, core, zl]
-            send(ref, ref, lgs.at[d - 1], lgr.at[d - 1], tp_dev(d))
+            send(ref, ref, lgs.at[to], lgr.at[t], (r, c, to))
 
     def last_wait():
-        for d in range(1, 8):
-            arrive(y.at[(7, *place(8 - d))], lgs.at[d - 1], lgr.at[d - 1])
+        for p in range(6, -1, -1):
+            by = peer(p)
+            arrive(y.at[(7, *place(by))], lgs.at[by], lgr.at[by])
 
     def rows_at(start):
         return (
@@ -417,8 +427,9 @@
             selw[:, :, cols].reshape(BLK, 256), piece, NT, preferred_element_type=F32
         )
     q[...] = (carried * SCALE_MODEL).astype(BF).reshape(8, SEL, TOK)
-    for d in range(1, 8):
-        send(q.at[lax.rem(t + d, 8)], qin.at[d - 1], qs.at[d - 1], qr.at[d - 1], tp_dev(d))
+    for p in range(7):
+        to = peer(p)
+        send(q.at[to], qin.at[t], qs.at[to], qr.at[t], (r, c, to))
 
     pick_pair(2)
     pick_pair(3)
@@ -430,16 +441,19 @@
         send(t2.at[lax.rem(x + d, 4)], t2x.at[d - 1], xs.at[d - 1], xr.at[d - 1], x_dev(d))
 
     total = q[t].astype(F32) + stt[...]
-    for d in range(1, 8):
-        arrive(qin.at[d - 1], qs.at[d - 1], qr.at[d - 1])
-        total = total + qin[d - 1].astype(F32)
+    for p in range(6, -1, -1):
+        by = peer(p)
+        arrive(qin.at[by], qs.at[by], qr.at[by])
+        total = total + qin[by].astype(F32)
     dy[t] = total.astype(BF)
-    for d in range(1, 8):
+    for p in range(7):
+        to = peer(p)
         ref = dy.at[t]
-        send(ref, ref, ds_.at[d - 1], dr_.at[d - 1], tp_dev(d))
+        send(ref, ref, ds_.at[to], dr_.at[t], (r, c, to))
     send_counts()
-    for d in range(1, 8):
-        arrive(dy.at[lax.rem(t + 8 - d, 8)], ds_.at[d - 1], dr_.at[d - 1])
+    for p in range(6, -1, -1):
+        by = peer(p)
+        arrive(dy.at[by], ds_.at[by], dr_.at[by])
     grad = jnp.dot(dy[...].reshape(BLK, TOK), act[...], preferred_element_type=F32) * SCALE_HIDDEN
     t1[...] = (factor * grad).astype(BF).reshape(8, SEL, HID)
 
@@ -527,12 +541,12 @@
         vmem((TOK, HID), BF), vmem((TOK, BLK), BF), vmem((TOK, HID), BF), vmem((TOK, BLK), BF),
         vmem((1, TOK), jnp.int32), vmem((8, 2, HID, HALF), BF), vmem((8, HID, BLK), BF),
         vmem((SEL, HID), F32), vmem((SEL, HID), F32),
-        vmem((8, 2, 4, SEL, BLK), BF), vmem((7, 4, SEL, BLK), BF), vmem((7, SEL, BLK), BF),
+        vmem((8, 2, 4, SEL, BLK), BF), vmem((7, 4, SEL, BLK), BF), vmem((8, SEL, BLK), BF),
         vmem((7, 4, SEL, BLK), BF), vmem((7, 3, SEL, BLK), BF),
         vmem((8, 2, 4, SEL, BLK), BF), vmem((2, 2, BLK, BLK), BF),
         vmem((TOK, HID), F32), vmem((TOK, HID), BF), vmem((8, SEL, HID), BF),
         vmem((8, SEL, TOK), BF), vmem((SEL, TOK), F32), vmem((SEL, HID), F32), vmem((SEL, HID), F32),
-        vmem((8, SEL, TOK), BF), vmem((7, SEL, TOK), BF), vmem((8, SEL, TOK), BF),
+        vmem((8, SEL, TOK), BF), vmem((8, SEL, TOK), BF), vmem((8, SEL, TOK), BF),
         vmem((8, SEL, HID), BF), vmem((7, SEL, HID), BF),
         vmem((4, 2, SEL, HID), BF), vmem((3, 2, SEL, HID), BF),
         vmem((SEL, HID), BF), vmem((SEL, HID), BF),
@@ -540,8 +554,8 @@
         dma((10,)),
         dma((2, 4, 2)), dma((2, 4, 2)), dma((2, 9)), dma((2, 9)), dma((2, 2, 2)), dma((2, 2, 2)),
         dma((7,)), dma((7,)), dma((7, 3)), dma((7, 3)), dma((7, 3)), dma((7, 3)), dma((7,)), dma((7,)),
-        dma((7,)), dma((7,)), dma((7,)), dma((7,)),
-        dma((7,)), dma((7,)), dma((7,)), dma((7,)), dma((7,)), dma((7,)),
+        dma((8,)), dma((8,)), dma((8,)), dma((8,)),
+        dma((8,)), dma((8,)), dma((8,)), dma((8,)), dma((7,)), dma((7,)),
         dma((3,)), dma((3,)), dma(()), dma(()), dma((7,)), dma((7,)), dma((7,)), dma((7,)),
     ]
     result = jax.ShapeDtypeStruct((SEL, HID), F32)

time: 92 us -> 92.6 us (level)
  no operation moved by 1% of the time
where the time goes in v5:
time: 92.6 us; the launch traced here: 92.5 us
  Pallas kernels  91.2 us (98%)
  between operations  1.29 us (1%)
    pallas_call x1, Pallas kernels, on_device(): pl.pallas_call(kernel, out_shape=(result,) * 4, in_specs=[whole] * 5 + [i...  90.3 us

profile of v5, /device:TPU:1, one launch (start us, length us, event | category | flops | bytes accessed | tf_op | source)
XLA Modules:
  0.0 92.5 jit_solution(2048767191773265406)
XLA Ops:
  1.3 90.3 %shard_map.129 = (f32[32,1024]{1,0:T(8,128)S(1)}, f32[32,1024]{1,0:T(8,128)S(1)}, f32[32,1024]{1,0:T(8,128)S(1)}, f32[32,1024]{1,0:T(8,128)S(1)}) custom-call(bf16[256,1024]{1,0:T(8,128)(2,1)} %bitcast.25, bf16[256,256]{1,0:T(8,128)(2,1)} %bitcast.29, bf16[256,1024]{1,0:T(8,128)(2,1)} %bitcast.26, bf16[256,256]{1,0:T(8,128)(2,1)} %bitcast.30, ...), custom_call_target="tpu_custom_call" | custom-call | flops 3000000000 | bytes 4000000 | tf_op jit(solution)/shard_map/pallas_call | solution.py:562
  91.6 0.8 shard_map.130

commit v6 on v4

--- a/solution.py
+++ b/solution.py
@@ -284,7 +284,7 @@
         pick_y(ahead(step), 2 * step, other_rows)
 
     def pick_w(n):
-        selw[n] = lax.dot_general(first_rows, w2g[n], NT, preferred_element_type=F32).astype(BF)
+        selw[n] = w2g[n][:, :HALF].T[:SEL]
 
     def product(values, n):
         return lax.dot_general(values, w2g[n], NT, preferred_element_type=F32)
@@ -378,10 +378,10 @@
 
     ring(7)
     last_out()
+    stage2(6)
     for way in range(2):
         far_wait(way, 2)
         far_send(way, 5)
-    stage2(6)
     stage3(3)
     stage3(4)
     stage4(3)

time: 92 us -> 92 us (level)
  no operation moved by 1% of the time
where the time goes in v6:
time: 92 us; the launch traced here: 91.9 us
  Pallas kernels  90.6 us (98%)
  between operations  1.29 us (1%)
    pallas_call x1, Pallas kernels, on_device(): pl.pallas_call(kernel, out_shape=(result,) * 4, in_specs=[whole] * 5 + [i...  89.8 us

profile of v6, /device:TPU:1, one launch (start us, length us, event | category | flops | bytes accessed | tf_op | source)
XLA Modules:
  0.0 91.9 jit_solution(14635040533574459780)
XLA Ops:
  1.3 89.8 %shard_map.129 = (f32[32,1024]{1,0:T(8,128)S(1)}, f32[32,1024]{1,0:T(8,128)S(1)}, f32[32,1024]{1,0:T(8,128)S(1)}, f32[32,1024]{1,0:T(8,128)S(1)}) custom-call(bf16[256,1024]{1,0:T(8,128)(2,1)} %bitcast.25, bf16[256,256]{1,0:T(8,128)(2,1)} %bitcast.29, bf16[256,1024]{1,0:T(8,128)(2,1)} %bitcast.26, bf16[256,256]{1,0:T(8,128)(2,1)} %bitcast.30, ...), custom_call_target="tpu_custom_call" | custom-call | flops 3000000000 | bytes 4000000 | tf_op jit(solution)/shard_map/pallas_call | solution.py:548
  91.0 0.8 shard_map.130
